TPU v7x, 512 devices: a whole 4x4x16 slice. The times are simulated.
512 devices in a mesh: row: 32 (over z, core), col: 16 (over y, x).
Axes of the slice: x: 4, y: 4, z: 16, core: 2. Of those that a mesh axis runs over, the one named last changes fastest.
Arguments:
- noise: bfloat16 [4096, 16384], P('row', 'col'), may hold values from -6 to 6
- data: bfloat16 [4096, 16384], P('col', 'row'), may hold values from -6 to 6
Outputs:
- targets: bfloat16 [4096, 16384], P('row', 'col')
- noise_potential: float32 [4096], P('row')
- data_potential: float32 [4096], P('col')
All inputs are finite; a program needn't handle non-finite values.
Results may differ from a plain program's by a relative error of at most 0.017.
Values may be sent and summed in bfloat16 or wider, within the bound.
No kernel may reach another device: no remote copies, remote signals or barrier semaphores. Data moves between devices by JAX's collectives and lax.ppermute only.
A program may use at most 64 MiB of HBM per device.

v0:
```python
import jax
import jax.numpy as jnp
from jax import lax
from jax.sharding import PartitionSpec as P

ITERS = 3


epsilon = 0.01


def body(noise, data):
    rows_here = noise.shape[0]
    cols_here = data.shape[0]
    log_rows = jnp.log(jnp.float32(rows_here * lax.axis_size("row")))
    log_cols = jnp.log(jnp.float32(cols_here * lax.axis_size("col")))
    noise_full = lax.all_gather(noise, "col", axis=1, tiled=True)
    width = noise_full.shape[1]
    noise_sq = jnp.einsum("id,id->i", noise_full, noise_full, preferred_element_type=jnp.float32)
    data_full = lax.all_gather(data, "row", axis=1, tiled=True)
    data_sq = jnp.einsum("jd,jd->j", data_full, data_full, preferred_element_type=jnp.float32)
    dots = lax.dot_general(
        noise_full, data_full, (((1,), (1,)), ((), ())), preferred_element_type=jnp.float32
    )
    cost = (noise_sq[:, None] + data_sq[None, :] - 2.0 * dots) / width
    data_potential = jnp.zeros((cols_here,), jnp.float32)
    noise_potential = jnp.zeros((rows_here,), jnp.float32)
    for step in range(ITERS):
        scores = (data_potential[None, :] - cost) / epsilon
        peak = lax.pmax(jnp.max(scores, axis=1), "col")
        total = lax.psum(jnp.sum(jnp.exp(scores - peak[:, None]), axis=1), "col")
        noise_potential = epsilon * (-log_rows - (peak + jnp.log(total)))
        scores = (noise_potential[:, None] - cost) / epsilon
        peak = lax.pmax(jnp.max(scores, axis=0), "row")
        total = lax.psum(jnp.sum(jnp.exp(scores - peak[None, :]), axis=0), "row")
        data_potential = epsilon * (-log_cols - (peak + jnp.log(total)))
    plan = jnp.exp(
        (noise_potential[:, None] + data_potential[None, :] - cost) / epsilon + log_rows
    ).astype(jnp.bfloat16)
    mass = lax.psum(jnp.sum(plan.astype(jnp.float32), axis=1), "col")
    partial_value = jnp.dot(plan, data_full, preferred_element_type=jnp.float32)
    weighted = lax.psum_scatter(
        partial_value.astype(jnp.bfloat16), "col", scatter_dimension=1, tiled=True
    ).astype(jnp.float32)
    targets = (weighted / mass[:, None]).astype(jnp.bfloat16)
    return (targets, noise_potential, data_potential)


def solution(mesh):
    return jax.shard_map(
        body,
        mesh=mesh,
        in_specs=(P("row", "col"), P("col", "row")),
        out_specs=(P("row", "col"), P("row"), P("col")),
        check_vma=False,
    )
```

profile of v0, /device:TPU:1, one launch (start us, length us, event | category | flops | bytes accessed | tf_op | source)
XLA Modules:
  0.0 773.5 jit_solution(14367036197075278122)
XLA Ops:
  7.2 0.7 all-gather.3.cloned.1.call-update
  7.9 0.7 all-gather.5.cloned.1.call-update
  8.7 74.6 %all-gather.3.cloned.1.call-done = bf16[128,16384]{1,0:T(8,128)(2,1)} async-done(((bf16[128,1024]{1,0:T(8,128)(2,1)}), bf16[128,16384]{1,0:T(8,128)(2,1)}) %all-gather.3.cloned.1.call-update) | async-done | bytes 4194320 | tf_op jit(solution)/shard_map/all_gather | solution.py:17
  83.3 3.1 fusion.1
  86.3 78.9 %all-gather.5.cloned.1.call-done = bf16[256,16384]{1,0:T(8,128)(2,1)} async-done(((bf16[256,512]{1,0:T(8,128)(2,1)}), bf16[256,16384]{1,0:T(8,128)(2,1)}) %all-gather.5.cloned.1.call-update) | async-done | bytes 8388624 | tf_op jit(solution)/shard_map/all_gather | solution.py:20
  165.2 5.3 fusion
  170.5 0.5 copy-done
  171.0 5.2 fusion.4
  176.2 33.2 %pmax.42 = f32[128]{0:T(128)S(1)} all-reduce(f32[128]{0:T(128)S(1)} %get-tuple-element.5), channel_id=1, replica_groups=mesh['row'=32,'col'=16] {'col'}, use_global_device_ids=true, to_apply=%region_1.0 | all-reduce | flops 128 | bytes 1024 | tf_op jit(solution)/shard_map/pmax | solution.py:30
  209.4 0.2 exponential_reduce_fusion.5
  209.6 28.8 %psum.49 = f32[128]{0:T(128)S(1)} all-reduce(f32[128]{0:T(128)S(1)} %exponential_reduce_fusion.5), channel_id=1, replica_groups=mesh['row'=32,'col'=16] {'col'}, use_global_device_ids=true, to_apply=%region_3.0 | all-reduce | flops 128 | bytes 1024 | tf_op jit(solution)/shard_map/psum | solution.py:31
  238.5 59.2 %pmax.43 = f32[256]{0:T(256)S(1)} all-reduce(f32[256]{0:T(256)S(1)} %fusion.5), channel_id=1, replica_groups=mesh['row'=32,'col'=16] {'row'}, use_global_device_ids=true, to_apply=%region_5.0 | all-reduce | flops 256 | bytes 2048 | tf_op jit(solution)/shard_map/pmax | solution.py:34
  297.7 0.1 exponential_reduce_fusion.4
  297.8 45.8 %psum.50 = f32[256]{0:T(256)S(1)} all-reduce(f32[256]{0:T(256)S(1)} %exponential_reduce_fusion.4), channel_id=1, replica_groups=mesh['row'=32,'col'=16] {'row'}, use_global_device_ids=true, to_apply=%region_7.0 | all-reduce | flops 256 | bytes 2048 | tf_op jit(solution)/shard_map/psum | solution.py:35
  343.6 0.1 fusion.6
  343.7 30.2 %pmax.44 = f32[128]{0:T(128)S(1)} all-reduce(f32[128]{0:T(128)S(1)} %fusion.6), channel_id=1, replica_groups=mesh['row'=32,'col'=16] {'col'}, use_global_device_ids=true, to_apply=%region_9.0 | all-reduce | flops 128 | bytes 1024 | tf_op jit(solution)/shard_map/pmax | solution.py:30
  374.0 0.2 exponential_reduce_fusion.3
  374.2 28.5 %psum.51 = f32[128]{0:T(128)S(1)} all-reduce(f32[128]{0:T(128)S(1)} %exponential_reduce_fusion.3), channel_id=1, replica_groups=mesh['row'=32,'col'=16] {'col'}, use_global_device_ids=true, to_apply=%region_11.0 | all-reduce | flops 128 | bytes 1024 | tf_op jit(solution)/shard_map/psum | solution.py:31
  402.8 60.0 %pmax.45 = f32[256]{0:T(256)S(1)} all-reduce(f32[256]{0:T(256)S(1)} %fusion.7), channel_id=1, replica_groups=mesh['row'=32,'col'=16] {'row'}, use_global_device_ids=true, to_apply=%region_13.0 | all-reduce | flops 256 | bytes 2048 | tf_op jit(solution)/shard_map/pmax | solution.py:34
  462.8 0.1 exponential_reduce_fusion.2
  462.9 45.8 %psum.52 = f32[256]{0:T(256)S(1)} all-reduce(f32[256]{0:T(256)S(1)} %exponential_reduce_fusion.2), channel_id=1, replica_groups=mesh['row'=32,'col'=16] {'row'}, use_global_device_ids=true, to_apply=%region_15.0 | all-reduce | flops 256 | bytes 2048 | tf_op jit(solution)/shard_map/psum | solution.py:35
  508.8 30.2 %pmax.46 = f32[128]{0:T(128)S(1)} all-reduce(f32[128]{0:T(128)S(1)} %fusion.8), channel_id=1, replica_groups=mesh['row'=32,'col'=16] {'col'}, use_global_device_ids=true, to_apply=%region_17.0 | all-reduce | flops 128 | bytes 1024 | tf_op jit(solution)/shard_map/pmax | solution.py:30
  539.1 0.2 exponential_reduce_fusion.1
  539.2 28.5 %psum.53 = f32[128]{0:T(128)S(1)} all-reduce(f32[128]{0:T(128)S(1)} %exponential_reduce_fusion.1), channel_id=1, replica_groups=mesh['row'=32,'col'=16] {'col'}, use_global_device_ids=true, to_apply=%region_19.0 | all-reduce | flops 128 | bytes 1024 | tf_op jit(solution)/shard_map/psum | solution.py:31
  567.9 60.0 %pmax.47 = f32[256]{0:T(256)S(1)} all-reduce(f32[256]{0:T(256)S(1)} %fusion.9), channel_id=1, replica_groups=mesh['row'=32,'col'=16] {'row'}, use_global_device_ids=true, to_apply=%region_21.0 | all-reduce | flops 256 | bytes 2048 | tf_op jit(solution)/shard_map/pmax | solution.py:34
  627.9 0.1 exponential_reduce_fusion
  628.0 45.8 %psum.54 = f32[256]{0:T(256)S(1)} all-reduce(f32[256]{0:T(256)S(1)} %exponential_reduce_fusion), channel_id=1, replica_groups=mesh['row'=32,'col'=16] {'row'}, use_global_device_ids=true, to_apply=%region_23.0 | all-reduce | flops 256 | bytes 2048 | tf_op jit(solution)/shard_map/psum | solution.py:35
  673.8 0.2 convert_reduce_fusion
  674.0 6.7 convolution_convert_fusion
  680.7 30.4 %psum.55 = f32[128]{0:T(128)S(1)} all-reduce(f32[128]{0:T(128)S(1)} %get-tuple-element.3), channel_id=1, replica_groups=mesh['row'=32,'col'=16] {'col'}, use_global_device_ids=true, to_apply=%region_26.0 | all-reduce | flops 128 | bytes 1024 | tf_op jit(solution)/shard_map/psum | solution.py:40
  711.1 54.1 %reduce-scatter.2.cloned.1.call-done = bf16[128,1024]{1,0:T(8,128)(2,1)} async-done(((bf16[128,16384]{1,0:T(8,128)(2,1)}), bf16[128,1024]{1,0:T(8,128)(2,1)}) %reduce-scatter.2.cloned.1.call-update) | async-done | bytes 262160 | tf_op jit(solution)/shard_map/reduce_scatter | solution.py:42
  765.2 1.8 divide_convert_fusion
  (19 shorter events, 0.6 us)
Async XLA Ops:
  7.2 76.1 %all-gather.3.cloned.1.call-start = ((), (), s32[]{:S(2)}) async-start(), calls=%async_computation.1 | async-start | bytes 4456448 | tf_op jit(solution)/shard_map/all_gather | solution.py:17
  7.9 157.3 %all-gather.5.cloned.1.call-start = ((), (), s32[]{:S(2)}) async-start(), calls=%async_computation.2 | async-start | bytes 8650752 | tf_op jit(solution)/shard_map/all_gather | solution.py:20
  8.6 756.6 %reduce-scatter.2.cloned.1.call-start = ((), (), s32[]{:S(2)}) async-start(), calls=%async_computation.3 | async-start | bytes 4456448 | tf_op jit(solution)/shard_map/reduce_scatter | solution.py:42
  165.2 5.8 copy-start
  567.8 112.9 %copy-start.1 = (f32[128]{0:T(128)}, f32[128]{0:T(128)S(1)}, u32[]{:S(2)}) copy-start(f32[128]{0:T(128)S(1)} %subtract_multiply_fusion.9) | copy-start | bytes 1540
  673.8 6.9 copy-start.2
Sparse Core Ops, SparseCore 0:
  11.0 72.2 all-gather.2
  85.4 79.7 all-gather.4
  680.8 84.3 reduce-scatter.1
where the time goes:
time: 775 us; the launch traced here: 774 us
  blocking collectives  527 us (68%)
  waiting for transfers between devices  209 us (27%)
  between operations  13.8 us (2%)
  other arithmetic  11.8 us (2%)
  matrix products  11.8 us (2%)
    pmax x3, blocking collectives, body(): peak = lax.pmax(jnp.max(scores, axis=0), 'row')  179 us
    psum x3, blocking collectives, body(): total = lax.psum(jnp.sum(jnp.exp(scores - peak[None, :]), axis=0), 'row')  137 us
    pmax x3, blocking collectives, body(): peak = lax.pmax(jnp.max(scores, axis=1), 'col')  93.7 us
    psum x3, blocking collectives, body(): total = lax.psum(jnp.sum(jnp.exp(scores - peak[:, None]), axis=1), 'col')  85.8 us
    all_gather x1, waiting for transfers between devices, body(): data_full = lax.all_gather(data, 'row', axis=1, tiled=True)  78.9 us
    all_gather x1, waiting for transfers between devices, body(): noise_full = lax.all_gather(noise, 'col', axis=1, tiled=True)  74.6 us
    reduce_scatter x1, waiting for transfers between devices, body(): lax.psum_scatter(partial_value.astype(jnp.bfloat16), 'col', scatter_dimen...  54.1 us
    psum x1, blocking collectives, body(): mass = lax.psum(jnp.sum(plan.astype(jnp.float32), axis=1), 'col')  30.4 us
  transfers between devices with their start and end apart: 3, of which 3 were waited for; matrix products, arithmetic and copies ran while one was open for 0% of the time, Pallas kernels for 0%

commit v1 on v0

v1 whole, which is shorter than its diff:
```python
import functools
import math

import jax
import jax.numpy as jnp
from jax import lax
from jax.experimental import pallas as pl
from jax.experimental.pallas import tpu as pltpu
from jax.sharding import PartitionSpec as P

ITERS = 3
EPS = 0.01
COLS = 16
ROWS = 32
F32 = jnp.float32
BF16 = jnp.bfloat16
GRID = 4
MIB = 1024 * 1024


def copies(value, axis, size):
    sent = jnp.broadcast_to(value[None], (size,) + value.shape)
    return lax.all_to_all(sent, axis, split_axis=0, concat_axis=0)


def fold(value):
    value = value.astype(F32)
    value = value * value
    parts = [value[..., k : k + 128] for k in range(0, value.shape[-1], 128)]
    while len(parts) > 1:
        parts = [parts[k] + parts[k + 1] for k in range(0, len(parts), 2)]
    return parts[0]


def split(value):
    parts = []
    for _ in range(2):
        far = value * 65537.0
        head = far - (far - value)
        parts.append(head)
        value = value - head
    return parts + [value]


def cost_kernel(scale, place_ref, noise_ref, data_ref, noise_sq_ref, cost_ref, pack_ref, dots_ref, data_sq_ref):
    step = pl.program_id(0)
    core, plane = place_ref[0], place_ref[1]
    blocks, rows, _ = noise_ref.shape
    depth = data_ref.shape[2]
    part = pack_ref.shape[1]

    @pl.when(step == 0)
    def _():
        dots_ref[...] = jnp.zeros_like(dots_ref)
        data_sq_ref[...] = jnp.zeros_like(data_sq_ref)

    dots, data_sq = dots_ref[...], data_sq_ref[...]
    for b in range(blocks):
        for k in range(2):
            data = data_ref[2 * b + k]
            noise = noise_ref[b, :, k * depth : (k + 1) * depth]
            dots += lax.dot_general(noise, data, (((1,), (1,)), ((), ())), preferred_element_type=F32)
            data_sq += fold(data)
        here = pl.ds(pl.multiple_of(plane * part, part), part)
        pack_ref[step * blocks + b, :, :depth] = data_ref[2 * b + core, here, :]
    dots_ref[...], data_sq_ref[...] = dots, data_sq

    @pl.when(step == pl.num_programs(0) - 1)
    def _():
        squares = jnp.sum(noise_sq_ref[...], axis=1, keepdims=True) + jnp.sum(data_sq.T, axis=0, keepdims=True)
        cost = squares - 2.0 * dots
        cost_ref[...] = cost
        scores = cost * scale
        peak = jnp.max(scores, axis=1, keepdims=True)
        local = peak + jnp.log(jnp.sum(jnp.exp(scores - peak), axis=1, keepdims=True))
        line = jnp.broadcast_to(local, (rows, 128)).T[:part, :]
        place = lax.broadcasted_iota(jnp.int32, line.shape, 0)
        head, middle, rest = split(line)
        tail = jnp.where(place == 0, head, jnp.where(place == 1, middle, rest)).astype(BF16)
        for c in range(pack_ref.shape[0]):
            pack_ref[c, :, depth:] = tail


def plan_kernel(plan_ref, data_ref, out_ref, acc_ref, mass_ref):
    step = pl.program_id(0)
    parts, cores, blocks, _, width = data_ref.shape

    @pl.when(step == 0)
    def _():
        acc_ref[...] = jnp.zeros_like(acc_ref)
        mass_ref[...] = jnp.zeros_like(mass_ref)

    for b in range(blocks):
        plan = plan_ref[b]
        mass_ref[...] += jnp.sum(plan.astype(F32), axis=1, keepdims=True)
        for k in range(cores):
            block = jnp.concatenate([data_ref[s, k, b] for s in range(parts)], axis=0)
            acc_ref[:, k * width : (k + 1) * width] += jnp.dot(plan, block, preferred_element_type=F32)

    @pl.when(step == pl.num_programs(0) - 1)
    def _():
        out_ref[...] = (acc_ref[...] / mass_ref[...]).astype(BF16)


def log_sum_exp(value, axis):
    peak = jnp.max(value, axis=axis, keepdims=True)
    return jnp.squeeze(peak, axis) + jnp.log(jnp.sum(jnp.exp(value - peak), axis=axis))


def body(noise, data):
    rows, width = noise.shape
    cols, depth = data.shape
    planes = ROWS // 2
    part = cols // planes
    log_rows = math.log(rows * ROWS)
    log_cols = math.log(cols * COLS)
    scale = -1.0 / (EPS * width * COLS)
    row = lax.axis_index("row").astype(jnp.int32)
    place = jnp.stack([lax.rem(row, 2), row // 2])

    data_all = lax.all_gather(data, "row", axis=0)
    noise_all = copies(noise, "col", COLS)
    noise_sq = fold(noise_all).sum(axis=0)
    data_all, noise_all, noise_sq = lax.optimization_barrier((data_all, noise_all, noise_sq))

    some = COLS // GRID
    cost, pack = pl.pallas_call(
        functools.partial(cost_kernel, scale),
        out_shape=[
            jax.ShapeDtypeStruct((rows, cols), F32),
            jax.ShapeDtypeStruct((COLS, part, depth + rows), BF16),
        ],
        grid_spec=pltpu.PrefetchScalarGridSpec(
            num_scalar_prefetch=1,
            grid=(GRID,),
            in_specs=[
                pl.BlockSpec((some, rows, width), lambda c, place: (c, 0, 0)),
                pl.BlockSpec((2 * some, cols, depth), lambda c, place: (c, 0, 0)),
                pl.BlockSpec((rows, 128), lambda c, place: (0, 0)),
            ],
            out_specs=[
                pl.BlockSpec((rows, cols), lambda c, place: (0, 0)),
                pl.BlockSpec((COLS, part, depth + rows), lambda c, place: (0, 0, 0)),
            ],
            scratch_shapes=[
                pltpu.VMEM((rows, cols), F32),
                pltpu.VMEM((cols, 128), F32),
            ],
        ),
        compiler_params=pltpu.CompilerParams(vmem_limit_bytes=48 * MIB),
        cost_estimate=pl.CostEstimate(
            flops=2 * rows * cols * COLS * width, bytes_accessed=12 * MIB, transcendentals=0
        ),
        name="cost",
    )(place, noise_all, data_all, noise_sq)
    scores = cost * scale
    pack = lax.all_to_all(pack, "col", split_axis=0, concat_axis=0)
    parts = pack[:, :3, depth:].astype(F32).sum(axis=1)

    values = lax.all_gather(pack[:, :, :depth], "row", axis=0).reshape(planes, 2, COLS, part, depth)

    for step in range(ITERS):
        if step > 0:
            parts = copies(log_sum_exp(scores + v[None, :], 1).reshape(1, rows), "col", COLS)
        u = -log_rows - log_sum_exp(parts.reshape(COLS, rows), 0)
        local = log_sum_exp(scores + u[:, None], 0)
        parts = copies(local.reshape(1, cols), "row", ROWS)
        v = -log_cols - log_sum_exp(parts, 0).reshape(cols)

    values, v = lax.optimization_barrier((values, v))
    plan = jnp.exp(scores + u[:, None] + v[None, :] + log_rows).astype(BF16)
    plan = copies(plan, "col", COLS)
    targets = pl.pallas_call(
        plan_kernel,
        grid=(GRID,),
        out_shape=jax.ShapeDtypeStruct((rows, width), BF16),
        in_specs=[
            pl.BlockSpec((some, rows, cols), lambda c: (c, 0, 0)),
            pl.BlockSpec((planes, 2, some, part, depth), lambda c: (0, 0, c, 0, 0)),
        ],
        out_specs=pl.BlockSpec((rows, width), lambda c: (0, 0)),
        scratch_shapes=[pltpu.VMEM((rows, width), F32), pltpu.VMEM((rows, 1), F32)],
        compiler_params=pltpu.CompilerParams(vmem_limit_bytes=48 * MIB),
        name="plan",
    )(plan, values)
    return (targets, EPS * u, EPS * v)


def solution(mesh):
    return jax.shard_map(
        body,
        mesh=mesh,
        in_specs=(P("row", "col"), P("col", "row")),
        out_specs=(P("row", "col"), P("row"), P("col")),
        check_vma=False,
    )
```

time: 775 us -> 232 us (0.30)
  blocking collectives: 527 us -> 90.2 us
  waiting for transfers between devices: 209 us -> 88.8 us
  Pallas kernels: 0 us -> 13.3 us
  starting transfers between devices: 0.11 us -> 12.1 us
  matrix products: 11.8 us -> 0 us
    pmax x6 -> x0, blocking collectives: 273 us -> none  [the longest x3 179 us: body(): peak = lax.pmax(jnp.max(scores, axis=0), 'row')]
    psum x7 -> x0, blocking collectives: 254 us -> none  [the longest x3 137 us: body(): total = lax.psum(jnp.sum(jnp.exp(scores - peak[None, :]), axis=0), 'row')]
    all_gather x2, waiting for transfers between devices: 153 us -> 18.8 us  [the longest x1 18.8 us: body(): data_all = lax.all_gather(data, 'row', axis=0)]
    all_to_all x0 -> x6, blocking collectives: none -> 90.2 us  [the longest x5 74.8 us: copies(): return lax.all_to_all(sent, axis, split_axis=0, concat_axis=0)]
    all_to_all x0 -> x2, waiting for transfers between devices: none -> 69.2 us  [copies(): return lax.all_to_all(sent, axis, split_axis=0, concat_axis=0)]
    reduce_scatter x1 -> x0, waiting for transfers between devices: 54.1 us -> none  [body(): lax.psum_scatter(partial_value.astype(jnp.bfloat16), 'col', scatter_dimen...]
    pallas_call x0 -> x2, Pallas kernels: none -> 13.3 us  [the longest x1 7.62 us: body(): pl.pallas_call(functools.partial(cost_kernel, scale), out_shape=[jax.Shap...]
    all_to_all x0 -> x2, starting transfers between devices: none -> 12 us  [copies(): return lax.all_to_all(sent, axis, split_axis=0, concat_axis=0)]
  transfers between devices with their start and end apart: 3 -> 4, of which waited for: 3 -> 3; matrix products, arithmetic and copies ran while one was open for 0% -> 4% of each run, Pallas kernels for 0% -> 0%
where the time goes in v1:
time: 232 us; the launch traced here: 231 us
  blocking collectives  90.2 us (39%)
  waiting for transfers between devices  88.8 us (38%)
  between operations  14.2 us (6%)
  Pallas kernels  13.3 us (6%)
  starting transfers between devices  12.1 us (5%)
  other arithmetic  6.86 us (3%)
  local copies, waits for them, and re-layouts  5.43 us (2%)
    all_to_all x5, blocking collectives, copies(): return lax.all_to_all(sent, axis, split_axis=0, concat_axis=0)  74.8 us
    all_to_all x2, waiting for transfers between devices, copies(): return lax.all_to_all(sent, axis, split_axis=0, concat_axis=0)  69.2 us
    all_gather x1, waiting for transfers between devices, body(): data_all = lax.all_gather(data, 'row', axis=0)  18.8 us
    all_to_all x1, blocking collectives, body(): pack = lax.all_to_all(pack, 'col', split_axis=0, concat_axis=0)  15.5 us
    all_to_all x2, starting transfers between devices, copies(): return lax.all_to_all(sent, axis, split_axis=0, concat_axis=0)  12 us
    pallas_call x1, Pallas kernels, body(): pl.pallas_call(functools.partial(cost_kernel, scale), out_shape=[jax.Shap...  7.62 us
    pallas_call x1, Pallas kernels, body(): pl.pallas_call(plan_kernel, grid=(GRID,), out_shape=jax.ShapeDtypeStruct(...  5.71 us
    broadcast_in_dim x7, local copies, waits for them, and re-layouts, copies(): sent = jnp.broadcast_to(value[None], (size,) + value.shape)  4.7 us
  transfers between devices with their start and end apart: 4, of which 3 were waited for; matrix products, arithmetic and copies ran while one was open for 4% of the time, Pallas kernels for 0%

profile of v1, /device:TPU:1, one launch (start us, length us, event | category | flops | bytes accessed | tf_op | source)
XLA Modules:
  0.0 230.9 jit_solution(11447850441895086507)
XLA Ops:
  7.2 0.7 all-gather.5.cloned.1.call-update
  7.9 3.4 %broadcast_in_dim.14 = bf16[16,128,1024]{2,1,0:T(8,128)(2,1)} broadcast(bf16[128,1024]{1,0:T(8,128)(2,1)} %param.2), dimensions={1,2} | broadcast | bytes 4456448 | tf_op jit(solution)/shard_map/broadcast_in_dim | solution.py:22
  11.3 7.6 %all-to-all-start = ((bf16[16,128,1024]{2,1,0:T(8,128)(2,1)}), bf16[16,128,1024]{2,1,0:T(8,128)(2,1)}, u32[]{:S(2)}, u32[]{:S(2)}) async-start(bf16[16,128,1024]{2,1,0:T(8,128)(2,1)} %broadcast_in_dim.14), calls=%async_computation | async-start | bytes 8388608 | tf_op jit(solution)/shard_map/all_to_all | solution.py:23
  19.1 53.3 %all-to-all-done.noise_ref = bf16[16,128,1024]{2,1,0:T(8,128)(2,1)} async-done(((bf16[16,128,1024]{2,1,0:T(8,128)(2,1)}), bf16[16,128,1024]{2,1,0:T(8,128)(2,1)}, u32[]{:S(2)}, u32[]{:S(2)}) %all-to-all-start) | async-done | bytes 4194336 | tf_op jit(solution)/shard_map/all_to_all | solution.py:23
  72.4 3.5 %convert_multiply_fusion = f32[16,128,1024]{2,1,0:T(8,128)S(1)} fusion(bf16[16,128,1024]{2,1,0:T(8,128)(2,1)} %all-to-all-done.noise_ref), kind=kLoop, calls=%fused_computation | loop fusion | flops 4194304 | bytes 12582912 | tf_op jit(solution)/shard_map/mul | solution.py:28
  75.9 0.4 fusion.2.noise_sq_ref
  76.3 18.8 %all-gather.5.cloned.1.call-done = bf16[8192,512]{1,0:T(8,128)(2,1)} async-done(((bf16[256,512]{1,0:T(8,128)(2,1)}), bf16[8192,512]{1,0:T(8,128)(2,1)}) %all-gather.5.cloned.1.call-update) | async-done | bytes 8388624 | tf_op jit(solution)/shard_map/all_gather | solution.py:121
  95.1 7.6 %cost.1 = (f32[128,256]{1,0:T(8,128)S(1)}, bf16[16,16,640]{2,1,0:T(8,128)(2,1)S(1)}) custom-call(s32[2]{0:T(128)S(1)} %pad_add_fusion.place_ref, bf16[16,128,1024]{2,1,0:T(8,128)(2,1)} %all-to-all-done.noise_ref, bf16[32,256,512]{2,1,0:T(8,128)(2,1)} %bitcast.9, f32[128,128]{1,0:T(8,128)S(1)} %fusion.2.noise_sq_ref), custom_call_target="tpu_custom_call" | custom-call | flops 1073741824 | bytes 12582912 | tf_op jit(solution)/shard_map/cost/pallas_call | solution.py:127
  102.7 15.5 %all_to_all.40 = bf16[16,16,640]{2,1,0:T(8,128)(2,1)S(1)} all-to-all(bf16[16,16,640]{2,1,0:T(8,128)(2,1)S(1)} %get-tuple-element.14), channel_id=1, replica_groups=mesh['row'=32,'col'=16] {'col'}, dimensions={0} | all-to-all | bytes 655360 | tf_op jit(solution)/shard_map/all_to_all | solution.py:157
  118.2 0.7 slice.49
  119.0 0.1 add_reduce_fusion.3
  119.1 0.1 exponential_reduce_fusion.4
  119.3 21.0 %all_to_all.41 = f32[32,1,256]{2,1,0:T(1,128)S(1)} all-to-all(f32[32,1,256]{2,1,0:T(1,128)S(1)} %broadcast_in_dim.15), channel_id=1, replica_groups=mesh['row'=32,'col'=16] {'row'}, dimensions={0} | all-to-all | bytes 65536 | tf_op jit(solution)/shard_map/all_to_all | solution.py:23
  140.4 0.1 add_reduce_fusion.2
  140.5 0.2 exponential_reduce_fusion.3
  140.7 9.0 %all_to_all.42 = f32[16,1,128]{2,1,0:T(1,128)S(1)} all-to-all(f32[16,1,128]{2,1,0:T(1,128)S(1)} %broadcast_in_dim.16), channel_id=1, replica_groups=mesh['row'=32,'col'=16] {'col'}, dimensions={0} | all-to-all | bytes 16384 | tf_op jit(solution)/shard_map/all_to_all | solution.py:23
  149.8 0.1 add_reduce_fusion.1
  149.9 0.1 exponential_reduce_fusion.2
  150.0 17.6 %all_to_all.43 = f32[32,1,256]{2,1,0:T(1,128)S(1)} all-to-all(f32[32,1,256]{2,1,0:T(1,128)S(1)} %broadcast_in_dim.17), channel_id=1, replica_groups=mesh['row'=32,'col'=16] {'row'}, dimensions={0} | all-to-all | bytes 65536 | tf_op jit(solution)/shard_map/all_to_all | solution.py:23
  167.7 0.1 add_reduce_fusion
  167.8 0.2 exponential_reduce_fusion.1
  168.0 9.9 %all_to_all.44 = f32[16,1,128]{2,1,0:T(1,128)S(1)} all-to-all(f32[16,1,128]{2,1,0:T(1,128)S(1)} %broadcast_in_dim.18), channel_id=1, replica_groups=mesh['row'=32,'col'=16] {'col'}, dimensions={0} | all-to-all | bytes 16384 | tf_op jit(solution)/shard_map/all_to_all | solution.py:23
  177.9 0.5 broadcast_multiply_fusion.2
  178.5 0.1 add_reduce_fusion.4
  178.6 0.1 exponential_reduce_fusion
  178.7 17.3 %all_to_all.45 = f32[32,1,256]{2,1,0:T(1,128)S(1)} all-to-all(f32[32,1,256]{2,1,0:T(1,128)S(1)} %broadcast_in_dim.19), channel_id=1, replica_groups=mesh['row'=32,'col'=16] {'row'}, dimensions={0} | all-to-all | bytes 65536 | tf_op jit(solution)/shard_map/all_to_all | solution.py:23
  196.2 0.1 exponential_convert_fusion
  196.3 1.2 broadcast_in_dim.20
  197.5 4.4 %all-to-all-start.7 = ((bf16[16,128,256]{2,1,0:T(8,128)(2,1)}), bf16[16,128,256]{2,1,0:T(8,128)(2,1)S(1)}, u32[]{:S(2)}, u32[]{:S(2)}) async-start(bf16[16,128,256]{2,1,0:T(8,128)(2,1)} %broadcast_in_dim.20), calls=%async_computation.7 | async-start | bytes 2097152 | tf_op jit(solution)/shard_map/all_to_all | solution.py:23
  201.9 0.6 broadcast_multiply_fusion.1
  202.4 15.9 %all-to-all-done.7.plan_ref = bf16[16,128,256]{2,1,0:T(8,128)(2,1)S(1)} async-done(((bf16[16,128,256]{2,1,0:T(8,128)(2,1)}), bf16[16,128,256]{2,1,0:T(8,128)(2,1)S(1)}, u32[]{:S(2)}, u32[]{:S(2)}) %all-to-all-start.7) | async-done | bytes 1048608 | tf_op jit(solution)/shard_map/all_to_all | solution.py:23
  218.4 5.7 %plan.1 = bf16[128,1024]{1,0:T(8,128)(2,1)} custom-call(bf16[16,128,256]{2,1,0:T(8,128)(2,1)S(1)} %all-to-all-done.7.plan_ref, bf16[16,2,16,16,512]{4,3,2,1,0:T(8,128)(2,1)} %bitcast.8), custom_call_target="tpu_custom_call" | custom-call | tf_op jit(solution)/shard_map/plan/pallas_call | solution.py:173
  (33 shorter events, 0.8 us)
Async XLA Ops:
  7.2 87.9 %all-gather.5.cloned.1.call-start = ((), (), s32[]{:S(2)}) async-start(), calls=%async_computation.8 | async-start | bytes 8650752 | tf_op jit(solution)/shard_map/all_gather | solution.py:121
  11.3 61.1 %all-to-all-start = ((bf16[16,128,1024]{2,1,0:T(8,128)(2,1)}), bf16[16,128,1024]{2,1,0:T(8,128)(2,1)}, u32[]{:S(2)}, u32[]{:S(2)}) async-start(bf16[16,128,1024]{2,1,0:T(8,128)(2,1)} %broadcast_in_dim.14), calls=%async_computation | async-start | bytes 8388608 | tf_op jit(solution)/shard_map/all_to_all | solution.py:23
  19.0 177.2 %all-gather.7.cloned.1.call-start = ((), (), s32[]{:S(2)}) async-start(), calls=%async_computation.9 | async-start | bytes 8650752 | tf_op jit(solution)/shard_map/all_gather | solution.py:160
  197.5 20.9 %all-to-all-start.7 = ((bf16[16,128,256]{2,1,0:T(8,128)(2,1)}), bf16[16,128,256]{2,1,0:T(8,128)(2,1)S(1)}, u32[]{:S(2)}, u32[]{:S(2)}) async-start(bf16[16,128,256]{2,1,0:T(8,128)(2,1)} %broadcast_in_dim.20), calls=%async_computation.7 | async-start | bytes 2097152 | tf_op jit(solution)/shard_map/all_to_all | solution.py:23
Sparse Core Ops, SparseCore 0:
  10.1 84.9 all-gather.4
  119.0 75.1 all-gather.6

commit v2 on v1

--- a/solution.py
+++ b/solution.py
@@ -45,7 +45,7 @@
 def cost_kernel(scale, place_ref, noise_ref, data_ref, noise_sq_ref, cost_ref, pack_ref, dots_ref, data_sq_ref):
     step = pl.program_id(0)
     core, plane = place_ref[0], place_ref[1]
-    blocks, rows, _ = noise_ref.shape
+    blocks, _, rows = noise_ref.shape
     depth = data_ref.shape[2]
     part = pack_ref.shape[1]
 
@@ -58,8 +58,8 @@
     for b in range(blocks):
         for k in range(2):
             data = data_ref[2 * b + k]
-            noise = noise_ref[b, :, k * depth : (k + 1) * depth]
-            dots += lax.dot_general(noise, data, (((1,), (1,)), ((), ())), preferred_element_type=F32)
+            noise = noise_ref[b, k * depth : (k + 1) * depth, :]
+            dots += jnp.dot(data, noise, preferred_element_type=F32)
             data_sq += fold(data)
         here = pl.ds(pl.multiple_of(plane * part, part), part)
         pack_ref[step * blocks + b, :, :depth] = data_ref[2 * b + core, here, :]
@@ -67,13 +67,13 @@
 
     @pl.when(step == pl.num_programs(0) - 1)
     def _():
-        squares = jnp.sum(noise_sq_ref[...], axis=1, keepdims=True) + jnp.sum(data_sq.T, axis=0, keepdims=True)
-        cost = squares - 2.0 * dots
-        cost_ref[...] = cost
-        scores = cost * scale
-        peak = jnp.max(scores, axis=1, keepdims=True)
-        local = peak + jnp.log(jnp.sum(jnp.exp(scores - peak), axis=1, keepdims=True))
-        line = jnp.broadcast_to(local, (rows, 128)).T[:part, :]
+        squares = jnp.sum(data_sq, axis=1, keepdims=True) + noise_sq_ref[...]
+        turned = squares - 2.0 * dots
+        cost_ref[...] = turned.T
+        scores = turned * scale
+        peak = jnp.max(scores, axis=0, keepdims=True)
+        local = peak + jnp.log(jnp.sum(jnp.exp(scores - peak), axis=0, keepdims=True))
+        line = jnp.broadcast_to(local, (part, rows))
         place = lax.broadcasted_iota(jnp.int32, line.shape, 0)
         head, middle, rest = split(line)
         tail = jnp.where(place == 0, head, jnp.where(place == 1, middle, rest)).astype(BF16)
@@ -81,21 +81,26 @@
             pack_ref[c, :, depth:] = tail
 
 
+def stage_kernel(data_ref, out_ref):
+    parts, cores, blocks, part, depth = data_ref.shape
+    for b in range(blocks):
+        for s in range(parts):
+            for k in range(cores):
+                out_ref[b, s * part : (s + 1) * part, k * depth : (k + 1) * depth] = data_ref[s, k, b]
+
+
 def plan_kernel(plan_ref, data_ref, out_ref, acc_ref, mass_ref):
     step = pl.program_id(0)
-    parts, cores, blocks, _, width = data_ref.shape
 
     @pl.when(step == 0)
     def _():
         acc_ref[...] = jnp.zeros_like(acc_ref)
         mass_ref[...] = jnp.zeros_like(mass_ref)
 
-    for b in range(blocks):
+    for b in range(plan_ref.shape[0]):
         plan = plan_ref[b]
         mass_ref[...] += jnp.sum(plan.astype(F32), axis=1, keepdims=True)
-        for k in range(cores):
-            block = jnp.concatenate([data_ref[s, k, b] for s in range(parts)], axis=0)
-            acc_ref[:, k * width : (k + 1) * width] += jnp.dot(plan, block, preferred_element_type=F32)
+        acc_ref[...] += jnp.dot(plan, data_ref[b], preferred_element_type=F32)
 
     @pl.when(step == pl.num_programs(0) - 1)
     def _():
@@ -119,8 +124,8 @@
     place = jnp.stack([lax.rem(row, 2), row // 2])
 
     data_all = lax.all_gather(data, "row", axis=0)
-    noise_all = copies(noise, "col", COLS)
-    noise_sq = fold(noise_all).sum(axis=0)
+    noise_all = copies(noise.T, "col", COLS)
+    noise_sq = jnp.sum(jnp.square(noise_all.astype(F32)), axis=(0, 1)).reshape(1, rows)
     data_all, noise_all, noise_sq = lax.optimization_barrier((data_all, noise_all, noise_sq))
 
     some = COLS // GRID
@@ -134,16 +139,16 @@
             num_scalar_prefetch=1,
             grid=(GRID,),
             in_specs=[
-                pl.BlockSpec((some, rows, width), lambda c, place: (c, 0, 0)),
+                pl.BlockSpec((some, width, rows), lambda c, place: (c, 0, 0)),
                 pl.BlockSpec((2 * some, cols, depth), lambda c, place: (c, 0, 0)),
-                pl.BlockSpec((rows, 128), lambda c, place: (0, 0)),
+                pl.BlockSpec((1, rows), lambda c, place: (0, 0)),
             ],
             out_specs=[
                 pl.BlockSpec((rows, cols), lambda c, place: (0, 0)),
                 pl.BlockSpec((COLS, part, depth + rows), lambda c, place: (0, 0, 0)),
             ],
             scratch_shapes=[
-                pltpu.VMEM((rows, cols), F32),
+                pltpu.VMEM((cols, rows), F32),
                 pltpu.VMEM((cols, 128), F32),
             ],
         ),
@@ -167,22 +172,33 @@
         parts = copies(local.reshape(1, cols), "row", ROWS)
         v = -log_cols - log_sum_exp(parts, 0).reshape(cols)
 
-    values, v = lax.optimization_barrier((values, v))
     plan = jnp.exp(scores + u[:, None] + v[None, :] + log_rows).astype(BF16)
-    plan = copies(plan, "col", COLS)
+    plan = jnp.broadcast_to(plan[None], (COLS, rows, cols))
+    values, plan = lax.optimization_barrier((values, plan))
+    plan = lax.all_to_all(plan, "col", split_axis=0, concat_axis=0)
+    staged = pl.pallas_call(
+        stage_kernel,
+        grid=(GRID,),
+        out_shape=jax.ShapeDtypeStruct((COLS, cols, width), BF16),
+        in_specs=[pl.BlockSpec((planes, 2, some, part, depth), lambda c: (0, 0, c, 0, 0))],
+        out_specs=pl.BlockSpec((some, cols, width), lambda c: (c, 0, 0)),
+        compiler_params=pltpu.CompilerParams(vmem_limit_bytes=50 * MIB),
+        cost_estimate=pl.CostEstimate(flops=0, bytes_accessed=16 * MIB, transcendentals=0),
+        name="stage",
+    )(values)
     targets = pl.pallas_call(
         plan_kernel,
         grid=(GRID,),
         out_shape=jax.ShapeDtypeStruct((rows, width), BF16),
         in_specs=[
             pl.BlockSpec((some, rows, cols), lambda c: (c, 0, 0)),
-            pl.BlockSpec((planes, 2, some, part, depth), lambda c: (0, 0, c, 0, 0)),
+            pl.BlockSpec((some, cols, width), lambda c: (c, 0, 0)),
         ],
         out_specs=pl.BlockSpec((rows, width), lambda c: (0, 0)),
         scratch_shapes=[pltpu.VMEM((rows, width), F32), pltpu.VMEM((rows, 1), F32)],
-        compiler_params=pltpu.CompilerParams(vmem_limit_bytes=48 * MIB),
+        compiler_params=pltpu.CompilerParams(vmem_limit_bytes=24 * MIB),
         name="plan",
-    )(plan, values)
+    )(plan, staged)
     return (targets, EPS * u, EPS * v)
 
 

time: 232 us -> 232 us (level)
  waiting for transfers between devices: 88.8 us -> 81.1 us
  Pallas kernels: 13.3 us -> 17.1 us
  local copies, waits for them, and re-layouts: 5.43 us -> 9.18 us
    all_to_all x2 -> x1, waiting for transfers between devices: 69.2 us -> 53.3 us  [copies(): return lax.all_to_all(sent, axis, split_axis=0, concat_axis=0)]
    all_to_all x0 -> x1, waiting for transfers between devices: none -> 9.28 us  [body(): plan = lax.all_to_all(plan, 'col', split_axis=0, concat_axis=0)]
    pallas_call x0 -> x1, Pallas kernels: none -> 7.08 us  [body(): pl.pallas_call(stage_kernel, grid=(GRID,), out_shape=jax.ShapeDtypeStruct...]
    all_to_all x2 -> x1, starting transfers between devices: 12 us -> 7.64 us  [copies(): return lax.all_to_all(sent, axis, split_axis=0, concat_axis=0)]
    reduce_sum x1, other arithmetic: 0.37 us -> 4.42 us  [body(): jnp.sum(jnp.square(noise_all.astype(F32)), axis=(0, 1)).reshape(1, rows)]
    all_to_all x0 -> x1, starting transfers between devices: none -> 3.73 us  [body(): plan = lax.all_to_all(plan, 'col', split_axis=0, concat_axis=0)]
    mul x1 -> x0, other arithmetic: 3.47 us -> none  [fold(): value = value * value]
    unnamed x0 -> x2, local copies, waits for them, and re-layouts: none -> 3.38 us
  transfers between devices with their start and end apart: 4 -> 4, of which waited for: 3 -> 3; matrix products, arithmetic and copies ran while one was open for 4% -> 5% of each run, Pallas kernels for 0% -> 3%
where the time goes in v2:
time: 232 us; the launch traced here: 231 us
  blocking collectives  90.2 us (39%)
  waiting for transfers between devices  81.1 us (35%)
  Pallas kernels  17.1 us (7%)
  between operations  14.2 us (6%)
  starting transfers between devices  11.4 us (5%)
  local copies, waits for them, and re-layouts  9.18 us (4%)
  other arithmetic  7.45 us (3%)
    all_to_all x5, blocking collectives, copies(): return lax.all_to_all(sent, axis, split_axis=0, concat_axis=0)  74.8 us
    all_to_all x1, waiting for transfers between devices, copies(): return lax.all_to_all(sent, axis, split_axis=0, concat_axis=0)  53.3 us
    all_gather x1, waiting for transfers between devices, body(): data_all = lax.all_gather(data, 'row', axis=0)  17.8 us
    all_to_all x1, blocking collectives, body(): pack = lax.all_to_all(pack, 'col', split_axis=0, concat_axis=0)  15.5 us
    all_to_all x1, waiting for transfers between devices, body(): plan = lax.all_to_all(plan, 'col', split_axis=0, concat_axis=0)  9.28 us
    all_to_all x1, starting transfers between devices, copies(): return lax.all_to_all(sent, axis, split_axis=0, concat_axis=0)  7.64 us
    pallas_call x1, Pallas kernels, body(): pl.pallas_call(functools.partial(cost_kernel, scale), out_shape=[jax.Shap...  7.27 us
    pallas_call x1, Pallas kernels, body(): pl.pallas_call(stage_kernel, grid=(GRID,), out_shape=jax.ShapeDtypeStruct...  7.08 us
  transfers between devices with their start and end apart: 4, of which 3 were waited for; matrix products, arithmetic and copies ran while one was open for 5% of the time, Pallas kernels for 3%

profile of v2, /device:TPU:1, one launch (start us, length us, event | category | flops | bytes accessed | tf_op | source)
XLA Modules:
  0.0 230.7 jit_solution(13232174902904035986)
XLA Ops:
  7.2 0.7 all-gather.5.cloned.1.call-update
  7.9 1.1 copy.17
  9.0 2.8 %broadcast_in_dim.14 = bf16[16,1024,128]{2,1,0:T(8,128)(2,1)} broadcast(bf16[1024,128]{1,0:T(8,128)(2,1)S(1)} %copy.17), dimensions={1,2} | broadcast | bytes 4456448 | tf_op jit(solution)/shard_map/broadcast_in_dim | solution.py:22
  11.8 7.6 %all-to-all-start = ((bf16[16,1024,128]{2,1,0:T(8,128)(2,1)}), bf16[16,1024,128]{2,1,0:T(8,128)(2,1)}, u32[]{:S(2)}, u32[]{:S(2)}) async-start(bf16[16,1024,128]{2,1,0:T(8,128)(2,1)} %broadcast_in_dim.14), calls=%async_computation | async-start | bytes 8388608 | tf_op jit(solution)/shard_map/all_to_all | solution.py:23
  19.6 53.3 %all-to-all-done.noise_ref = bf16[16,1024,128]{2,1,0:T(8,128)(2,1)} async-done(((bf16[16,1024,128]{2,1,0:T(8,128)(2,1)}), bf16[16,1024,128]{2,1,0:T(8,128)(2,1)}, u32[]{:S(2)}, u32[]{:S(2)}) %all-to-all-start) | async-done | bytes 4194336 | tf_op jit(solution)/shard_map/all_to_all | solution.py:23
  72.9 4.4 %multiply_reduce_fusion = f32[128]{0:T(128)S(1)} fusion(bf16[16,1024,128]{2,1,0:T(8,128)(2,1)} %all-to-all-done.noise_ref), kind=kLoop, calls=%fused_computation | loop fusion | flops 6291328 | bytes 4194816 | tf_op jit(solution)/shard_map/reduce_sum | solution.py:128
  77.3 17.8 %all-gather.5.cloned.1.call-done = bf16[8192,512]{1,0:T(8,128)(2,1)} async-done(((bf16[256,512]{1,0:T(8,128)(2,1)}), bf16[8192,512]{1,0:T(8,128)(2,1)}) %all-gather.5.cloned.1.call-update) | async-done | bytes 8388624 | tf_op jit(solution)/shard_map/all_gather | solution.py:126
  95.1 7.3 %cost.1 = (f32[128,256]{1,0:T(8,128)S(1)}, bf16[16,16,640]{2,1,0:T(8,128)(2,1)S(1)}) custom-call(s32[2]{0:T(128)S(1)} %pad_add_fusion.place_ref, bf16[16,1024,128]{2,1,0:T(8,128)(2,1)} %all-to-all-done.noise_ref, bf16[32,256,512]{2,1,0:T(8,128)(2,1)} %bitcast.11, f32[1,128]{1,0:T(1,128)S(1)} %bitcast.10), custom_call_target="tpu_custom_call" | custom-call | flops 1073741824 | bytes 12582912 | tf_op jit(solution)/shard_map/cost/pallas_call | solution.py:132
  102.4 15.5 %all_to_all.40 = bf16[16,16,640]{2,1,0:T(8,128)(2,1)S(1)} all-to-all(bf16[16,16,640]{2,1,0:T(8,128)(2,1)S(1)} %get-tuple-element.13), channel_id=1, replica_groups=mesh['row'=32,'col'=16] {'col'}, dimensions={0} | all-to-all | bytes 655360 | tf_op jit(solution)/shard_map/all_to_all | solution.py:162
  117.8 0.7 slice.8
  118.7 0.1 add_reduce_fusion.3
  118.8 0.1 exponential_reduce_fusion.4
  118.9 21.0 %all_to_all.41 = f32[32,1,256]{2,1,0:T(1,128)S(1)} all-to-all(f32[32,1,256]{2,1,0:T(1,128)S(1)} %broadcast_in_dim.15), channel_id=1, replica_groups=mesh['row'=32,'col'=16] {'row'}, dimensions={0} | all-to-all | bytes 65536 | tf_op jit(solution)/shard_map/all_to_all | solution.py:23
  140.0 0.1 add_reduce_fusion.2
  140.1 0.2 exponential_reduce_fusion.3
  140.3 9.0 %all_to_all.42 = f32[16,1,128]{2,1,0:T(1,128)S(1)} all-to-all(f32[16,1,128]{2,1,0:T(1,128)S(1)} %broadcast_in_dim.16), channel_id=1, replica_groups=mesh['row'=32,'col'=16] {'col'}, dimensions={0} | all-to-all | bytes 16384 | tf_op jit(solution)/shard_map/all_to_all | solution.py:23
  149.4 0.1 add_reduce_fusion.1
  149.5 0.1 exponential_reduce_fusion.2
  149.7 17.6 %all_to_all.43 = f32[32,1,256]{2,1,0:T(1,128)S(1)} all-to-all(f32[32,1,256]{2,1,0:T(1,128)S(1)} %broadcast_in_dim.17), channel_id=1, replica_groups=mesh['row'=32,'col'=16] {'row'}, dimensions={0} | all-to-all | bytes 65536 | tf_op jit(solution)/shard_map/all_to_all | solution.py:23
  167.3 0.1 add_reduce_fusion
  167.5 0.2 exponential_reduce_fusion.1
  167.7 9.9 %all_to_all.44 = f32[16,1,128]{2,1,0:T(1,128)S(1)} all-to-all(f32[16,1,128]{2,1,0:T(1,128)S(1)} %broadcast_in_dim.18), channel_id=1, replica_groups=mesh['row'=32,'col'=16] {'col'}, dimensions={0} | all-to-all | bytes 16384 | tf_op jit(solution)/shard_map/all_to_all | solution.py:23
  177.6 0.5 broadcast_multiply_fusion.2
  178.2 0.1 exponential_reduce_fusion
  178.4 17.3 %all_to_all.45 = f32[32,1,256]{2,1,0:T(1,128)S(1)} all-to-all(f32[32,1,256]{2,1,0:T(1,128)S(1)} %broadcast_in_dim.19), channel_id=1, replica_groups=mesh['row'=32,'col'=16] {'row'}, dimensions={0} | all-to-all | bytes 65536 | tf_op jit(solution)/shard_map/all_to_all | solution.py:23
  195.8 0.6 broadcast_multiply_fusion.1
  196.5 1.1 broadcast_in_dim.20
  197.6 3.7 %all-to-all-start.7 = ((bf16[16,128,256]{2,1,0:T(8,128)(2,1)}), bf16[16,128,256]{2,1,0:T(8,128)(2,1)S(1)}, u32[]{:S(2)}, u32[]{:S(2)}) async-start(bf16[16,128,256]{2,1,0:T(8,128)(2,1)} %broadcast_in_dim.20), calls=%async_computation.7 | async-start | bytes 2097152 | tf_op jit(solution)/shard_map/all_to_all | solution.py:178
  201.4 7.1 %stage.1.data_ref = bf16[16,256,1024]{2,1,0:T(8,128)(2,1)} custom-call(bf16[16,2,16,16,512]{4,3,2,1,0:T(8,128)(2,1)} %bitcast.12), custom_call_target="tpu_custom_call" | custom-call | bytes 16777216 | tf_op jit(solution)/shard_map/stage/pallas_call | solution.py:179
  208.4 9.3 %all-to-all-done.7.plan_ref = bf16[16,128,256]{2,1,0:T(8,128)(2,1)S(1)} async-done(((bf16[16,128,256]{2,1,0:T(8,128)(2,1)}), bf16[16,128,256]{2,1,0:T(8,128)(2,1)S(1)}, u32[]{:S(2)}, u32[]{:S(2)}) %all-to-all-start.7) | async-done | bytes 1048608 | tf_op jit(solution)/shard_map/all_to_all | solution.py:178
  217.7 3.4 %copy-done = bf16[16,256,1024]{2,1,0:T(8,128)(2,1)S(1)} copy-done((bf16[16,256,1024]{2,1,0:T(8,128)(2,1)S(1)}, bf16[16,256,1024]{2,1,0:T(8,128)(2,1)}, u32[]{:S(2)}) %copy-start) | copy-done | bytes 8388632
  221.1 2.7 %plan.1 = bf16[128,1024]{1,0:T(8,128)(2,1)} custom-call(bf16[16,128,256]{2,1,0:T(8,128)(2,1)S(1)} %all-to-all-done.7.plan_ref, bf16[16,256,1024]{2,1,0:T(8,128)(2,1)S(1)} %copy-done), custom_call_target="tpu_custom_call" | custom-call | tf_op jit(solution)/shard_map/plan/pallas_call | solution.py:189
  (35 shorter events, 1.0 us)
Async XLA Ops:
  7.2 87.9 %all-gather.5.cloned.1.call-start = ((), (), s32[]{:S(2)}) async-start(), calls=%async_computation.8 | async-start | bytes 8650752 | tf_op jit(solution)/shard_map/all_gather | solution.py:126
  11.8 61.1 %all-to-all-start = ((bf16[16,1024,128]{2,1,0:T(8,128)(2,1)}), bf16[16,1024,128]{2,1,0:T(8,128)(2,1)}, u32[]{:S(2)}, u32[]{:S(2)}) async-start(bf16[16,1024,128]{2,1,0:T(8,128)(2,1)} %broadcast_in_dim.14), calls=%async_computation | async-start | bytes 8388608 | tf_op jit(solution)/shard_map/all_to_all | solution.py:23
  19.4 177.1 %all-gather.7.cloned.1.call-start = ((), (), s32[]{:S(2)}) async-start(), calls=%async_computation.9 | async-start | bytes 8650752 | tf_op jit(solution)/shard_map/all_gather | solution.py:165
  197.6 20.1 %all-to-all-start.7 = ((bf16[16,128,256]{2,1,0:T(8,128)(2,1)}), bf16[16,128,256]{2,1,0:T(8,128)(2,1)S(1)}, u32[]{:S(2)}, u32[]{:S(2)}) async-start(bf16[16,128,256]{2,1,0:T(8,128)(2,1)} %broadcast_in_dim.20), calls=%async_computation.7 | async-start | bytes 2097152 | tf_op jit(solution)/shard_map/all_to_all | solution.py:178
  217.7 3.4 %copy-start = (bf16[16,256,1024]{2,1,0:T(8,128)(2,1)S(1)}, bf16[16,256,1024]{2,1,0:T(8,128)(2,1)}, u32[]{:S(2)}) copy-start(bf16[16,256,1024]{2,1,0:T(8,128)(2,1)} %stage.1.data_ref) | copy-start | bytes 25165828
Sparse Core Ops, SparseCore 0:
  10.1 84.9 all-gather.4
  118.7 75.1 all-gather.6

commit v3 on v2

--- a/solution.py
+++ b/solution.py
@@ -16,6 +16,7 @@
 BF16 = jnp.bfloat16
 GRID = 4
 MIB = 1024 * 1024
+VM = pl.BlockSpec(memory_space=pltpu.VMEM)
 
 
 def copies(value, axis, size):
@@ -45,7 +46,7 @@
 def cost_kernel(scale, place_ref, noise_ref, data_ref, noise_sq_ref, cost_ref, pack_ref, dots_ref, data_sq_ref):
     step = pl.program_id(0)
     core, plane = place_ref[0], place_ref[1]
-    blocks, _, rows = noise_ref.shape
+    blocks, rows = data_ref.shape[0] // 2, noise_ref.shape[2]
     depth = data_ref.shape[2]
     part = pack_ref.shape[1]
 
@@ -58,7 +59,7 @@
     for b in range(blocks):
         for k in range(2):
             data = data_ref[2 * b + k]
-            noise = noise_ref[b, k * depth : (k + 1) * depth, :]
+            noise = noise_ref[step * blocks + b, k * depth : (k + 1) * depth, :]
             dots += jnp.dot(data, noise, preferred_element_type=F32)
             data_sq += fold(data)
         here = pl.ds(pl.multiple_of(plane * part, part), part)
@@ -89,22 +90,15 @@
                 out_ref[b, s * part : (s + 1) * part, k * depth : (k + 1) * depth] = data_ref[s, k, b]
 
 
-def plan_kernel(plan_ref, data_ref, out_ref, acc_ref, mass_ref):
-    step = pl.program_id(0)
-
-    @pl.when(step == 0)
-    def _():
-        acc_ref[...] = jnp.zeros_like(acc_ref)
-        mass_ref[...] = jnp.zeros_like(mass_ref)
-
-    for b in range(plan_ref.shape[0]):
-        plan = plan_ref[b]
-        mass_ref[...] += jnp.sum(plan.astype(F32), axis=1, keepdims=True)
-        acc_ref[...] += jnp.dot(plan, data_ref[b], preferred_element_type=F32)
-
-    @pl.when(step == pl.num_programs(0) - 1)
-    def _():
-        out_ref[...] = (acc_ref[...] / mass_ref[...]).astype(BF16)
+def plan_kernel(plan_ref, data_ref, out_ref):
+    _, rows, _ = plan_ref.shape
+    acc = jnp.zeros(out_ref.shape, F32)
+    mass = jnp.zeros((rows, 1), F32)
+    for c in range(plan_ref.shape[0]):
+        plan = plan_ref[c]
+        mass += jnp.sum(plan.astype(F32), axis=1, keepdims=True)
+        acc += jnp.dot(plan, data_ref[c], preferred_element_type=F32)
+    out_ref[...] = (acc / mass).astype(BF16)
 
 
 def log_sum_exp(value, axis):
@@ -139,7 +133,7 @@
             num_scalar_prefetch=1,
             grid=(GRID,),
             in_specs=[
-                pl.BlockSpec((some, width, rows), lambda c, place: (c, 0, 0)),
+                VM,
                 pl.BlockSpec((2 * some, cols, depth), lambda c, place: (c, 0, 0)),
                 pl.BlockSpec((1, rows), lambda c, place: (0, 0)),
             ],
@@ -182,20 +176,15 @@
         out_shape=jax.ShapeDtypeStruct((COLS, cols, width), BF16),
         in_specs=[pl.BlockSpec((planes, 2, some, part, depth), lambda c: (0, 0, c, 0, 0))],
         out_specs=pl.BlockSpec((some, cols, width), lambda c: (c, 0, 0)),
-        compiler_params=pltpu.CompilerParams(vmem_limit_bytes=50 * MIB),
+        compiler_params=pltpu.CompilerParams(vmem_limit_bytes=42 * MIB),
         cost_estimate=pl.CostEstimate(flops=0, bytes_accessed=16 * MIB, transcendentals=0),
         name="stage",
     )(values)
     targets = pl.pallas_call(
         plan_kernel,
-        grid=(GRID,),
         out_shape=jax.ShapeDtypeStruct((rows, width), BF16),
-        in_specs=[
-            pl.BlockSpec((some, rows, cols), lambda c: (c, 0, 0)),
-            pl.BlockSpec((some, cols, width), lambda c: (c, 0, 0)),
-        ],
-        out_specs=pl.BlockSpec((rows, width), lambda c: (0, 0)),
-        scratch_shapes=[pltpu.VMEM((rows, width), F32), pltpu.VMEM((rows, 1), F32)],
+        in_specs=[VM, VM],
+        out_specs=VM,
         compiler_params=pltpu.CompilerParams(vmem_limit_bytes=24 * MIB),
         name="plan",
     )(plan, staged)

time: 232 us -> 231 us (level)
  local copies, waits for them, and re-layouts: 9.18 us -> 12.5 us
  Pallas kernels: 17.1 us -> 13.9 us
    unnamed x2 -> x4, local copies, waits for them, and re-layouts: 3.38 us -> 6.6 us
    pallas_call x1, Pallas kernels: 7.08 us -> 4.27 us  [body(): pl.pallas_call(stage_kernel, grid=(GRID,), out_shape=jax.ShapeDtypeStruct...]
  transfers between devices with their start and end apart: 4 -> 4, of which waited for: 3 -> 3; matrix products, arithmetic and copies ran while one was open for 5% -> 5% of each run, Pallas kernels for 3% -> 2%
where the time goes in v3:
time: 231 us; the launch traced here: 230 us
  blocking collectives  90.2 us (39%)
  waiting for transfers between devices  80.7 us (35%)
  between operations  14.2 us (6%)
  Pallas kernels  13.9 us (6%)
  local copies, waits for them, and re-layouts  12.5 us (5%)
  starting transfers between devices  11.4 us (5%)
  other arithmetic  7.45 us (3%)
    all_to_all x5, blocking collectives, copies(): return lax.all_to_all(sent, axis, split_axis=0, concat_axis=0)  74.8 us
    all_to_all x1, waiting for transfers between devices, copies(): return lax.all_to_all(sent, axis, split_axis=0, concat_axis=0)  53.3 us
    all_gather x1, waiting for transfers between devices, body(): data_all = lax.all_gather(data, 'row', axis=0)  17.8 us
    all_to_all x1, blocking collectives, body(): pack = lax.all_to_all(pack, 'col', split_axis=0, concat_axis=0)  15.5 us
    all_to_all x1, waiting for transfers between devices, body(): plan = lax.all_to_all(plan, 'col', split_axis=0, concat_axis=0)  8.86 us
    all_to_all x1, starting transfers between devices, copies(): return lax.all_to_all(sent, axis, split_axis=0, concat_axis=0)  7.64 us
    pallas_call x1, Pallas kernels, body(): pl.pallas_call(functools.partial(cost_kernel, scale), out_shape=[jax.Shap...  7.63 us
    unnamed x4, local copies, waits for them, and re-layouts  6.6 us
  transfers between devices with their start and end apart: 4, of which 3 were waited for; matrix products, arithmetic and copies ran while one was open for 5% of the time, Pallas kernels for 2%

profile of v3, /device:TPU:1, one launch (start us, length us, event | category | flops | bytes accessed | tf_op | source)
XLA Modules:
  0.0 230.4 jit_solution(14197001530402230567)
XLA Ops:
  7.2 0.7 all-gather.5.cloned.1.call-update
  7.9 1.1 copy.17
  9.0 2.8 %broadcast_in_dim.14 = bf16[16,1024,128]{2,1,0:T(8,128)(2,1)} broadcast(bf16[1024,128]{1,0:T(8,128)(2,1)S(1)} %copy.17), dimensions={1,2} | broadcast | bytes 4456448 | tf_op jit(solution)/shard_map/broadcast_in_dim | solution.py:23
  11.8 7.6 %all-to-all-start = ((bf16[16,1024,128]{2,1,0:T(8,128)(2,1)}), bf16[16,1024,128]{2,1,0:T(8,128)(2,1)}, u32[]{:S(2)}, u32[]{:S(2)}) async-start(bf16[16,1024,128]{2,1,0:T(8,128)(2,1)} %broadcast_in_dim.14), calls=%async_computation | async-start | bytes 8388608 | tf_op jit(solution)/shard_map/all_to_all | solution.py:24
  19.6 53.3 %all-to-all-done.noise_ref = bf16[16,1024,128]{2,1,0:T(8,128)(2,1)} async-done(((bf16[16,1024,128]{2,1,0:T(8,128)(2,1)}), bf16[16,1024,128]{2,1,0:T(8,128)(2,1)}, u32[]{:S(2)}, u32[]{:S(2)}) %all-to-all-start) | async-done | bytes 4194336 | tf_op jit(solution)/shard_map/all_to_all | solution.py:24
  72.9 4.4 %multiply_reduce_fusion = f32[128]{0:T(128)S(1)} fusion(bf16[16,1024,128]{2,1,0:T(8,128)(2,1)} %all-to-all-done.noise_ref), kind=kLoop, calls=%fused_computation | loop fusion | flops 6291328 | bytes 4194816 | tf_op jit(solution)/shard_map/reduce_sum | solution.py:122
  77.3 17.8 %all-gather.5.cloned.1.call-done = bf16[8192,512]{1,0:T(8,128)(2,1)} async-done(((bf16[256,512]{1,0:T(8,128)(2,1)}), bf16[8192,512]{1,0:T(8,128)(2,1)}) %all-gather.5.cloned.1.call-update) | async-done | bytes 8388624 | tf_op jit(solution)/shard_map/all_gather | solution.py:120
  95.1 7.6 %cost.1 = (f32[128,256]{1,0:T(8,128)S(1)}, bf16[16,16,640]{2,1,0:T(8,128)(2,1)S(1)}) custom-call(s32[2]{0:T(128)S(1)} %pad_add_fusion.place_ref, bf16[16,1024,128]{2,1,0:T(8,128)(2,1)} %all-to-all-done.noise_ref, bf16[32,256,512]{2,1,0:T(8,128)(2,1)} %bitcast.11, f32[1,128]{1,0:T(1,128)S(1)} %bitcast.10), custom_call_target="tpu_custom_call" | custom-call | flops 1073741824 | bytes 12582912 | tf_op jit(solution)/shard_map/cost/pallas_call | solution.py:126
  102.7 15.5 %all_to_all.40 = bf16[16,16,640]{2,1,0:T(8,128)(2,1)S(1)} all-to-all(bf16[16,16,640]{2,1,0:T(8,128)(2,1)S(1)} %get-tuple-element.13), channel_id=1, replica_groups=mesh['row'=32,'col'=16] {'col'}, dimensions={0} | all-to-all | bytes 655360 | tf_op jit(solution)/shard_map/all_to_all | solution.py:156
  118.2 0.7 slice.8
  119.1 0.1 exponential_reduce_fusion.4
  119.3 21.0 %all_to_all.41 = f32[32,1,256]{2,1,0:T(1,128)S(1)} all-to-all(f32[32,1,256]{2,1,0:T(1,128)S(1)} %broadcast_in_dim.15), channel_id=1, replica_groups=mesh['row'=32,'col'=16] {'row'}, dimensions={0} | all-to-all | bytes 65536 | tf_op jit(solution)/shard_map/all_to_all | solution.py:24
  140.4 0.1 add_reduce_fusion.2
  140.5 0.2 exponential_reduce_fusion.3
  140.7 9.0 %all_to_all.42 = f32[16,1,128]{2,1,0:T(1,128)S(1)} all-to-all(f32[16,1,128]{2,1,0:T(1,128)S(1)} %broadcast_in_dim.16), channel_id=1, replica_groups=mesh['row'=32,'col'=16] {'col'}, dimensions={0} | all-to-all | bytes 16384 | tf_op jit(solution)/shard_map/all_to_all | solution.py:24
  149.8 0.1 add_reduce_fusion.1
  149.9 0.1 exponential_reduce_fusion.2
  150.0 17.6 %all_to_all.43 = f32[32,1,256]{2,1,0:T(1,128)S(1)} all-to-all(f32[32,1,256]{2,1,0:T(1,128)S(1)} %broadcast_in_dim.17), channel_id=1, replica_groups=mesh['row'=32,'col'=16] {'row'}, dimensions={0} | all-to-all | bytes 65536 | tf_op jit(solution)/shard_map/all_to_all | solution.py:24
  167.7 0.1 add_reduce_fusion
  167.8 0.2 exponential_reduce_fusion.1
  168.0 9.9 %all_to_all.44 = f32[16,1,128]{2,1,0:T(1,128)S(1)} all-to-all(f32[16,1,128]{2,1,0:T(1,128)S(1)} %broadcast_in_dim.18), channel_id=1, replica_groups=mesh['row'=32,'col'=16] {'col'}, dimensions={0} | all-to-all | bytes 16384 | tf_op jit(solution)/shard_map/all_to_all | solution.py:24
  178.0 0.5 broadcast_multiply_fusion.2
  178.6 0.1 exponential_reduce_fusion
  178.7 17.3 %all_to_all.45 = f32[32,1,256]{2,1,0:T(1,128)S(1)} all-to-all(f32[32,1,256]{2,1,0:T(1,128)S(1)} %broadcast_in_dim.19), channel_id=1, replica_groups=mesh['row'=32,'col'=16] {'row'}, dimensions={0} | all-to-all | bytes 65536 | tf_op jit(solution)/shard_map/all_to_all | solution.py:24
  196.2 0.6 broadcast_multiply_fusion.1
  196.9 1.2 broadcast_in_dim.20
  198.1 3.7 %all-to-all-start.7 = ((bf16[16,128,256]{2,1,0:T(8,128)(2,1)}), bf16[16,128,256]{2,1,0:T(8,128)(2,1)S(1)}, u32[]{:S(2)}, u32[]{:S(2)}) async-start(bf16[16,128,256]{2,1,0:T(8,128)(2,1)} %broadcast_in_dim.20), calls=%async_computation.7 | async-start | bytes 2097152 | tf_op jit(solution)/shard_map/all_to_all | solution.py:172
  201.8 4.3 %stage.1.data_ref = bf16[16,256,1024]{2,1,0:T(8,128)(2,1)S(1)} custom-call(bf16[16,2,16,16,512]{4,3,2,1,0:T(8,128)(2,1)} %bitcast.12), custom_call_target="tpu_custom_call" | custom-call | bytes 16777216 | tf_op jit(solution)/shard_map/stage/pallas_call | solution.py:173
  206.1 3.2 %copy-done = bf16[16,256,1024]{2,1,0:T(8,128)(2,1)} copy-done((bf16[16,256,1024]{2,1,0:T(8,128)(2,1)}, bf16[16,256,1024]{2,1,0:T(8,128)(2,1)S(1)}, u32[]{:S(2)}) %copy-start) | copy-done | bytes 8388632
  209.3 8.9 %all-to-all-done.7.plan_ref = bf16[16,128,256]{2,1,0:T(8,128)(2,1)S(1)} async-done(((bf16[16,128,256]{2,1,0:T(8,128)(2,1)}), bf16[16,128,256]{2,1,0:T(8,128)(2,1)S(1)}, u32[]{:S(2)}, u32[]{:S(2)}) %all-to-all-start.7) | async-done | bytes 1048608 | tf_op jit(solution)/shard_map/all_to_all | solution.py:172
  218.2 3.4 %copy-done.1 = bf16[16,256,1024]{2,1,0:T(8,128)(2,1)S(1)} copy-done((bf16[16,256,1024]{2,1,0:T(8,128)(2,1)S(1)}, bf16[16,256,1024]{2,1,0:T(8,128)(2,1)}, u32[]{:S(2)}) %copy-start.1) | copy-done | bytes 8388632
  221.5 2.0 plan.1
  (37 shorter events, 1.1 us)
Async XLA Ops:
  7.2 87.9 %all-gather.5.cloned.1.call-start = ((), (), s32[]{:S(2)}) async-start(), calls=%async_computation.8 | async-start | bytes 8650752 | tf_op jit(solution)/shard_map/all_gather | solution.py:120
  11.8 61.1 %all-to-all-start = ((bf16[16,1024,128]{2,1,0:T(8,128)(2,1)}), bf16[16,1024,128]{2,1,0:T(8,128)(2,1)}, u32[]{:S(2)}, u32[]{:S(2)}) async-start(bf16[16,1024,128]{2,1,0:T(8,128)(2,1)} %broadcast_in_dim.14), calls=%async_computation | async-start | bytes 8388608 | tf_op jit(solution)/shard_map/all_to_all | solution.py:24
  19.4 177.4 %all-gather.7.cloned.1.call-start = ((), (), s32[]{:S(2)}) async-start(), calls=%async_computation.9 | async-start | bytes 8650752 | tf_op jit(solution)/shard_map/all_gather | solution.py:159
  198.1 20.1 %all-to-all-start.7 = ((bf16[16,128,256]{2,1,0:T(8,128)(2,1)}), bf16[16,128,256]{2,1,0:T(8,128)(2,1)S(1)}, u32[]{:S(2)}, u32[]{:S(2)}) async-start(bf16[16,128,256]{2,1,0:T(8,128)(2,1)} %broadcast_in_dim.20), calls=%async_computation.7 | async-start | bytes 2097152 | tf_op jit(solution)/shard_map/all_to_all | solution.py:172
  206.1 3.2 %copy-start = (bf16[16,256,1024]{2,1,0:T(8,128)(2,1)}, bf16[16,256,1024]{2,1,0:T(8,128)(2,1)S(1)}, u32[]{:S(2)}) copy-start(bf16[16,256,1024]{2,1,0:T(8,128)(2,1)S(1)} %stage.1.data_ref) | copy-start | bytes 25165828
  218.2 3.4 %copy-start.1 = (bf16[16,256,1024]{2,1,0:T(8,128)(2,1)S(1)}, bf16[16,256,1024]{2,1,0:T(8,128)(2,1)}, u32[]{:S(2)}) copy-start(bf16[16,256,1024]{2,1,0:T(8,128)(2,1)} %copy-done) | copy-start | bytes 25165828
Sparse Core Ops, SparseCore 0:
  10.1 84.9 all-gather.4
  119.1 75.1 all-gather.6

commit v4 on v1

v4 whole, which is shorter than its diff:
```python
import functools
import math

import jax
import jax.numpy as jnp
from jax import lax
from jax.experimental import pallas as pl
from jax.experimental.pallas import tpu as pltpu
from jax.sharding import PartitionSpec as P

ITERS = 3
EPS = 0.01
COLS = 16
ROWS = 32
F32 = jnp.float32
BF16 = jnp.bfloat16
PARTS = 8
MIB = 1024 * 1024
VM = pl.BlockSpec(memory_space=pltpu.VMEM)
SM = pl.BlockSpec(memory_space=pltpu.SMEM)
ANY = pl.BlockSpec(memory_space=pl.ANY)


def copies(value, axis, size):
    sent = jnp.broadcast_to(value[None], (size,) + value.shape)
    return lax.all_to_all(sent, axis, split_axis=0, concat_axis=0)


def fold(value):
    value = value.astype(F32)
    value = value * value
    parts = [value[..., k : k + 128] for k in range(0, value.shape[-1], 128)]
    while len(parts) > 1:
        parts = [parts[k] + parts[k + 1] for k in range(0, len(parts), 2)]
    return parts[0]


def split(value):
    parts = []
    for _ in range(2):
        far = value * 65537.0
        head = far - (far - value)
        parts.append(head)
        value = value - head
    return parts + [value]


def cost_kernel(scale, place_ref, noise_hbm, data_hbm, noise_sq_ref, cost_ref, pack_ref, noise_ref, data_ref, sems):
    core, plane = place_ref[0], place_ref[1]
    blocks, _, rows = noise_ref.shape
    _, cols, depth = data_ref.shape
    part = pack_ref.shape[1]
    some = blocks // PARTS
    copies_in = []
    for k in range(PARTS):
        pair = []
        for n, (source, target, size) in enumerate(((noise_hbm, noise_ref, some), (data_hbm, data_ref, 2 * some))):
            here = pl.ds(k * size, size)
            pair.append(pltpu.make_async_copy(source.at[here], target.at[here], sems.at[n, k]))
            pair[-1].start()
        copies_in.append(pair)

    share = pl.ds(pl.multiple_of(plane * part, part), part)
    dots = jnp.zeros((cols, rows), F32)
    data_sq = jnp.zeros((cols, 128), F32)
    for k in range(PARTS):
        for copy in copies_in[k]:
            copy.wait()
        for b in range(k * some, (k + 1) * some):
            for half in range(2):
                data = data_ref[2 * b + half]
                noise = noise_ref[b, half * depth : (half + 1) * depth, :]
                dots += jnp.dot(data, noise, preferred_element_type=F32)
                data_sq += fold(data)
            pack_ref[b, :, :depth] = data_ref[2 * b + core, share, :]

    squares = jnp.sum(data_sq, axis=1, keepdims=True) + noise_sq_ref[...]
    turned = squares - 2.0 * dots
    cost_ref[...] = turned.T
    scores = turned * scale
    peak = jnp.max(scores, axis=0, keepdims=True)
    local = peak + jnp.log(jnp.sum(jnp.exp(scores - peak), axis=0, keepdims=True))
    line = jnp.broadcast_to(local, (part, rows))
    place = lax.broadcasted_iota(jnp.int32, line.shape, 0)
    head, middle, rest = split(line)
    tail = jnp.where(place == 0, head, jnp.where(place == 1, middle, rest)).astype(BF16)
    for c in range(blocks):
        pack_ref[c, :, depth:] = tail


def plan_kernel(plan_ref, data_hbm, out_ref, data_ref, acc_ref, sems):
    parts, cores, blocks, _, width = data_ref.shape
    rows = plan_ref.shape[1]
    some = blocks // PARTS
    copies_in = []
    for k in range(PARTS):
        here = pl.ds(k * some, some)
        copies_in.append(pltpu.make_async_copy(data_hbm.at[:, :, here], data_ref.at[:, :, here], sems.at[k]))
        copies_in[-1].start()
    acc_ref[...] = jnp.zeros_like(acc_ref)
    mass = jnp.zeros((rows, 1), F32)
    for b in range(blocks):
        mass += jnp.sum(plan_ref[b].astype(F32), axis=1, keepdims=True)
    for k in range(PARTS):
        copies_in[k].wait()
        for b in range(k * some, (k + 1) * some):
            for c in range(cores):
                block = jnp.concatenate([data_ref[s, c, b] for s in range(parts)], axis=0)
                acc_ref[:, c * width : (c + 1) * width] += jnp.dot(plan_ref[b], block, preferred_element_type=F32)
    out_ref[...] = (acc_ref[...] / mass).astype(BF16)


def log_sum_exp(value, axis):
    peak = jnp.max(value, axis=axis, keepdims=True)
    return jnp.squeeze(peak, axis) + jnp.log(jnp.sum(jnp.exp(value - peak), axis=axis))


def body(noise, data):
    rows, width = noise.shape
    cols, depth = data.shape
    planes = ROWS // 2
    part = cols // planes
    log_rows = math.log(rows * ROWS)
    log_cols = math.log(cols * COLS)
    scale = -1.0 / (EPS * width * COLS)
    row = lax.axis_index("row").astype(jnp.int32)
    place = jnp.stack([lax.rem(row, 2), row // 2])

    data_all = lax.all_gather(data, "row", axis=0)
    noise_all = copies(noise.T, "col", COLS)
    noise_sq = jnp.sum(jnp.square(noise_all.astype(F32)), axis=(0, 1)).reshape(1, rows)
    data_all, noise_all, noise_sq = lax.optimization_barrier((data_all, noise_all, noise_sq))

    cost, pack = pl.pallas_call(
        functools.partial(cost_kernel, scale),
        out_shape=[
            jax.ShapeDtypeStruct((rows, cols), F32),
            jax.ShapeDtypeStruct((COLS, part, depth + rows), BF16),
        ],
        in_specs=[SM, ANY, ANY, VM],
        out_specs=[VM, VM],
        scratch_shapes=[
            pltpu.VMEM((COLS, width, rows), BF16),
            pltpu.VMEM((2 * COLS, cols, depth), BF16),
            pltpu.SemaphoreType.DMA((2, PARTS)),
        ],
        compiler_params=pltpu.CompilerParams(vmem_limit_bytes=50 * MIB),
        cost_estimate=pl.CostEstimate(
            flops=2 * rows * cols * COLS * width, bytes_accessed=12 * MIB, transcendentals=0
        ),
        name="cost",
    )(place, noise_all, data_all, noise_sq)
    scores = cost * scale
    pack = lax.all_to_all(pack, "col", split_axis=0, concat_axis=0)
    parts = pack[:, :3, depth:].astype(F32).sum(axis=1)

    values = lax.all_gather(pack[:, :, :depth], "row", axis=0).reshape(planes, 2, COLS, part, depth)

    for step in range(ITERS):
        if step > 0:
            parts = copies(log_sum_exp(scores + v[None, :], 1).reshape(1, rows), "col", COLS)
        u = -log_rows - log_sum_exp(parts.reshape(COLS, rows), 0)
        local = log_sum_exp(scores + u[:, None], 0)
        parts = copies(local.reshape(1, cols), "row", ROWS)
        v = -log_cols - log_sum_exp(parts, 0).reshape(cols)

    values, v = lax.optimization_barrier((values, v))
    plan = jnp.exp(scores + u[:, None] + v[None, :] + log_rows).astype(BF16)
    plan = copies(plan, "col", COLS)
    targets = pl.pallas_call(
        plan_kernel,
        out_shape=jax.ShapeDtypeStruct((rows, width), BF16),
        in_specs=[VM, ANY],
        out_specs=VM,
        scratch_shapes=[
            pltpu.VMEM((planes, 2, COLS, part, depth), BF16),
            pltpu.VMEM((rows, width), F32),
            pltpu.SemaphoreType.DMA((PARTS,)),
        ],
        compiler_params=pltpu.CompilerParams(vmem_limit_bytes=50 * MIB),
        name="plan",
    )(plan, values)
    return (targets, EPS * u, EPS * v)


def solution(mesh):
    return jax.shard_map(
        body,
        mesh=mesh,
        in_specs=(P("row", "col"), P("col", "row")),
        out_specs=(P("row", "col"), P("row"), P("col")),
        check_vma=False,
    )
```

time: 232 us -> 229 us (0.987)
  Pallas kernels: 13.3 us -> 10.4 us
    reduce_sum x1, other arithmetic: 0.37 us -> 4.42 us  [body(): jnp.sum(jnp.square(noise_all.astype(F32)), axis=(0, 1)).reshape(1, rows)]
    mul x1 -> x0, other arithmetic: 3.47 us -> none  [fold(): value = value * value]
  transfers between devices with their start and end apart: 4 -> 4, of which waited for: 3 -> 3; matrix products, arithmetic and copies ran while one was open for 4% -> 5% of each run, Pallas kernels for 0% -> 0%
where the time goes in v4:
time: 229 us; the launch traced here: 228 us
  blocking collectives  90.2 us (39%)
  waiting for transfers between devices  87.7 us (38%)
  between operations  14.2 us (6%)
  starting transfers between devices  12.1 us (5%)
  Pallas kernels  10.4 us (5%)
  other arithmetic  7.45 us (3%)
  local copies, waits for them, and re-layouts  5.88 us (3%)
    all_to_all x5, blocking collectives, copies(): return lax.all_to_all(sent, axis, split_axis=0, concat_axis=0)  74.8 us
    all_to_all x2, waiting for transfers between devices, copies(): return lax.all_to_all(sent, axis, split_axis=0, concat_axis=0)  69.2 us
    all_gather x1, waiting for transfers between devices, body(): data_all = lax.all_gather(data, 'row', axis=0)  17.8 us
    all_to_all x1, blocking collectives, body(): pack = lax.all_to_all(pack, 'col', split_axis=0, concat_axis=0)  15.5 us
    all_to_all x2, starting transfers between devices, copies(): return lax.all_to_all(sent, axis, split_axis=0, concat_axis=0)  12 us
    pallas_call x1, Pallas kernels, body(): pl.pallas_call(functools.partial(cost_kernel, scale), out_shape=[jax.Shap...  5.9 us
  transfers between devices with their start and end apart: 4, of which 3 were waited for; matrix products, arithmetic and copies ran while one was open for 5% of the time, Pallas kernels for 0%

profile of v4, /device:TPU:1, one launch (start us, length us, event | category | flops | bytes accessed | tf_op | source)
XLA Modules:
  0.0 228.0 jit_solution(12537423223792483882)
XLA Ops:
  7.2 0.7 all-gather.5.cloned.1.call-update
  7.9 1.1 copy.17
  9.0 2.8 %broadcast_in_dim.14 = bf16[16,1024,128]{2,1,0:T(8,128)(2,1)} broadcast(bf16[1024,128]{1,0:T(8,128)(2,1)S(1)} %copy.17), dimensions={1,2} | broadcast | bytes 4456448 | tf_op jit(solution)/shard_map/broadcast_in_dim | solution.py:25
  11.8 7.6 %all-to-all-start = ((bf16[16,1024,128]{2,1,0:T(8,128)(2,1)}), bf16[16,1024,128]{2,1,0:T(8,128)(2,1)}, u32[]{:S(2)}, u32[]{:S(2)}) async-start(bf16[16,1024,128]{2,1,0:T(8,128)(2,1)} %broadcast_in_dim.14), calls=%async_computation | async-start | bytes 8388608 | tf_op jit(solution)/shard_map/all_to_all | solution.py:26
  19.6 53.3 %all-to-all-done.noise_hbm = bf16[16,1024,128]{2,1,0:T(8,128)(2,1)} async-done(((bf16[16,1024,128]{2,1,0:T(8,128)(2,1)}), bf16[16,1024,128]{2,1,0:T(8,128)(2,1)}, u32[]{:S(2)}, u32[]{:S(2)}) %all-to-all-start) | async-done | bytes 4194336 | tf_op jit(solution)/shard_map/all_to_all | solution.py:26
  72.9 4.4 %multiply_reduce_fusion = f32[128]{0:T(128)S(1)} fusion(bf16[16,1024,128]{2,1,0:T(8,128)(2,1)} %all-to-all-done.noise_hbm), kind=kLoop, calls=%fused_computation | loop fusion | flops 6291328 | bytes 4194816 | tf_op jit(solution)/shard_map/reduce_sum | solution.py:131
  77.3 17.8 %all-gather.5.cloned.1.call-done = bf16[8192,512]{1,0:T(8,128)(2,1)} async-done(((bf16[256,512]{1,0:T(8,128)(2,1)}), bf16[8192,512]{1,0:T(8,128)(2,1)}) %all-gather.5.cloned.1.call-update) | async-done | bytes 8388624 | tf_op jit(solution)/shard_map/all_gather | solution.py:129
  95.1 5.9 %cost.1 = (f32[128,256]{1,0:T(8,128)S(1)}, bf16[16,16,640]{2,1,0:T(8,128)(2,1)S(1)}) custom-call(s32[2]{0:T(128)S(1)} %pad_add_fusion.place_ref, bf16[16,1024,128]{2,1,0:T(8,128)(2,1)} %all-to-all-done.noise_hbm, bf16[32,256,512]{2,1,0:T(8,128)(2,1)} %bitcast.12, f32[1,128]{1,0:T(1,128)S(1)} %bitcast.10), custom_call_target="tpu_custom_call" | custom-call | flops 1073741824 | bytes 12582912 | tf_op jit(solution)/shard_map/cost/pallas_call | solution.py:134
  101.0 15.5 %all_to_all.40 = bf16[16,16,640]{2,1,0:T(8,128)(2,1)S(1)} all-to-all(bf16[16,16,640]{2,1,0:T(8,128)(2,1)S(1)} %get-tuple-element.14), channel_id=1, replica_groups=mesh['row'=32,'col'=16] {'col'}, dimensions={0} | all-to-all | bytes 655360 | tf_op jit(solution)/shard_map/all_to_all | solution.py:154
  116.4 0.7 slice.9
  117.3 0.1 add_reduce_fusion.3
  117.4 0.1 exponential_reduce_fusion.4
  117.6 21.0 %all_to_all.41 = f32[32,1,256]{2,1,0:T(1,128)S(1)} all-to-all(f32[32,1,256]{2,1,0:T(1,128)S(1)} %broadcast_in_dim.15), channel_id=1, replica_groups=mesh['row'=32,'col'=16] {'row'}, dimensions={0} | all-to-all | bytes 65536 | tf_op jit(solution)/shard_map/all_to_all | solution.py:26
  138.6 0.1 add_reduce_fusion.2
  138.7 0.2 exponential_reduce_fusion.3
  139.0 9.0 %all_to_all.42 = f32[16,1,128]{2,1,0:T(1,128)S(1)} all-to-all(f32[16,1,128]{2,1,0:T(1,128)S(1)} %broadcast_in_dim.16), channel_id=1, replica_groups=mesh['row'=32,'col'=16] {'col'}, dimensions={0} | all-to-all | bytes 16384 | tf_op jit(solution)/shard_map/all_to_all | solution.py:26
  148.1 0.1 add_reduce_fusion.1
  148.2 0.1 exponential_reduce_fusion.2
  148.3 17.6 %all_to_all.43 = f32[32,1,256]{2,1,0:T(1,128)S(1)} all-to-all(f32[32,1,256]{2,1,0:T(1,128)S(1)} %broadcast_in_dim.17), channel_id=1, replica_groups=mesh['row'=32,'col'=16] {'row'}, dimensions={0} | all-to-all | bytes 65536 | tf_op jit(solution)/shard_map/all_to_all | solution.py:26
  166.0 0.1 add_reduce_fusion
  166.1 0.2 exponential_reduce_fusion.1
  166.3 9.9 %all_to_all.44 = f32[16,1,128]{2,1,0:T(1,128)S(1)} all-to-all(f32[16,1,128]{2,1,0:T(1,128)S(1)} %broadcast_in_dim.18), channel_id=1, replica_groups=mesh['row'=32,'col'=16] {'col'}, dimensions={0} | all-to-all | bytes 16384 | tf_op jit(solution)/shard_map/all_to_all | solution.py:26
  176.2 0.5 broadcast_multiply_fusion.2
  176.8 0.1 add_reduce_fusion.4
  176.9 0.1 exponential_reduce_fusion
  177.0 17.3 %all_to_all.45 = f32[32,1,256]{2,1,0:T(1,128)S(1)} all-to-all(f32[32,1,256]{2,1,0:T(1,128)S(1)} %broadcast_in_dim.19), channel_id=1, replica_groups=mesh['row'=32,'col'=16] {'row'}, dimensions={0} | all-to-all | bytes 65536 | tf_op jit(solution)/shard_map/all_to_all | solution.py:26
  194.5 0.1 exponential_convert_fusion
  194.6 1.2 broadcast_in_dim.20
  195.8 4.4 %all-to-all-start.7 = ((bf16[16,128,256]{2,1,0:T(8,128)(2,1)}), bf16[16,128,256]{2,1,0:T(8,128)(2,1)S(1)}, u32[]{:S(2)}, u32[]{:S(2)}) async-start(bf16[16,128,256]{2,1,0:T(8,128)(2,1)} %broadcast_in_dim.20), calls=%async_computation.7 | async-start | bytes 2097152 | tf_op jit(solution)/shard_map/all_to_all | solution.py:26
  200.2 0.6 broadcast_multiply_fusion.1
  200.7 15.9 %all-to-all-done.7.plan_ref = bf16[16,128,256]{2,1,0:T(8,128)(2,1)S(1)} async-done(((bf16[16,128,256]{2,1,0:T(8,128)(2,1)}), bf16[16,128,256]{2,1,0:T(8,128)(2,1)S(1)}, u32[]{:S(2)}, u32[]{:S(2)}) %all-to-all-start.7) | async-done | bytes 1048608 | tf_op jit(solution)/shard_map/all_to_all | solution.py:26
  216.7 4.5 %plan.1 = bf16[128,1024]{1,0:T(8,128)(2,1)} custom-call(bf16[16,128,256]{2,1,0:T(8,128)(2,1)S(1)} %all-to-all-done.7.plan_ref, bf16[16,2,16,16,512]{4,3,2,1,0:T(8,128)(2,1)} %bitcast.11), custom_call_target="tpu_custom_call" | custom-call | tf_op jit(solution)/shard_map/plan/pallas_call | solution.py:170
  (33 shorter events, 0.8 us)
Async XLA Ops:
  7.2 87.9 %all-gather.5.cloned.1.call-start = ((), (), s32[]{:S(2)}) async-start(), calls=%async_computation.8 | async-start | bytes 8650752 | tf_op jit(solution)/shard_map/all_gather | solution.py:129
  11.8 61.1 %all-to-all-start = ((bf16[16,1024,128]{2,1,0:T(8,128)(2,1)}), bf16[16,1024,128]{2,1,0:T(8,128)(2,1)}, u32[]{:S(2)}, u32[]{:S(2)}) async-start(bf16[16,1024,128]{2,1,0:T(8,128)(2,1)} %broadcast_in_dim.14), calls=%async_computation | async-start | bytes 8388608 | tf_op jit(solution)/shard_map/all_to_all | solution.py:26
  19.4 175.0 %all-gather.7.cloned.1.call-start = ((), (), s32[]{:S(2)}) async-start(), calls=%async_computation.9 | async-start | bytes 8650752 | tf_op jit(solution)/shard_map/all_gather | solution.py:157
  195.8 20.9 %all-to-all-start.7 = ((bf16[16,128,256]{2,1,0:T(8,128)(2,1)}), bf16[16,128,256]{2,1,0:T(8,128)(2,1)S(1)}, u32[]{:S(2)}, u32[]{:S(2)}) async-start(bf16[16,128,256]{2,1,0:T(8,128)(2,1)} %broadcast_in_dim.20), calls=%async_computation.7 | async-start | bytes 2097152 | tf_op jit(solution)/shard_map/all_to_all | solution.py:26
Sparse Core Ops, SparseCore 0:
  10.1 84.9 all-gather.4
  117.3 75.1 all-gather.6

commit v5 on v4

--- a/solution.py
+++ b/solution.py
@@ -95,7 +95,8 @@
     copies_in = []
     for k in range(PARTS):
         here = pl.ds(k * some, some)
-        copies_in.append(pltpu.make_async_copy(data_hbm.at[:, :, here], data_ref.at[:, :, here], sems.at[k]))
+        source = data_hbm.at[:, :, here, :, pl.ds(0, width)]
+        copies_in.append(pltpu.make_async_copy(source, data_ref.at[:, :, here], sems.at[k]))
         copies_in[-1].start()
     acc_ref[...] = jnp.zeros_like(acc_ref)
     mass = jnp.zeros((rows, 1), F32)
@@ -154,7 +155,7 @@
     pack = lax.all_to_all(pack, "col", split_axis=0, concat_axis=0)
     parts = pack[:, :3, depth:].astype(F32).sum(axis=1)
 
-    values = lax.all_gather(pack[:, :, :depth], "row", axis=0).reshape(planes, 2, COLS, part, depth)
+    values = lax.all_gather(pack, "row", axis=0).reshape(planes, 2, COLS, part, depth + rows)
 
     for step in range(ITERS):
         if step > 0:
@@ -164,9 +165,10 @@
         parts = copies(local.reshape(1, cols), "row", ROWS)
         v = -log_cols - log_sum_exp(parts, 0).reshape(cols)
 
-    values, v = lax.optimization_barrier((values, v))
     plan = jnp.exp(scores + u[:, None] + v[None, :] + log_rows).astype(BF16)
-    plan = copies(plan, "col", COLS)
+    plan = jnp.broadcast_to(plan[None], (COLS, rows, cols))
+    values, _ = lax.optimization_barrier((values, plan))
+    plan = lax.all_to_all(plan, "col", split_axis=0, concat_axis=0)
     targets = pl.pallas_call(
         plan_kernel,
         out_shape=jax.ShapeDtypeStruct((rows, width), BF16),

time: 229 us -> 228 us (level)
    all_to_all x2 -> x1, waiting for transfers between devices: 69.2 us -> 53.3 us  [copies(): return lax.all_to_all(sent, axis, split_axis=0, concat_axis=0)]
    all_to_all x0 -> x1, waiting for transfers between devices: none -> 15.9 us  [body(): plan = lax.all_to_all(plan, 'col', split_axis=0, concat_axis=0)]
    all_to_all x2 -> x1, starting transfers between devices: 12 us -> 7.64 us  [copies(): return lax.all_to_all(sent, axis, split_axis=0, concat_axis=0)]
    all_to_all x0 -> x1, starting transfers between devices: none -> 3.85 us  [body(): plan = lax.all_to_all(plan, 'col', split_axis=0, concat_axis=0)]
  transfers between devices with their start and end apart: 4 -> 4, of which waited for: 3 -> 3; matrix products, arithmetic and copies ran while one was open for 5% -> 6% of each run, Pallas kernels for 0% -> 0%
where the time goes in v5:
time: 228 us; the launch traced here: 227 us
  blocking collectives  89.8 us (39%)
  waiting for transfers between devices  87.6 us (38%)
  between operations  14.2 us (6%)
  starting transfers between devices  11.6 us (5%)
  Pallas kernels  10.5 us (5%)
  other arithmetic  8.21 us (4%)
  local copies, waits for them, and re-layouts  5.05 us (2%)
    all_to_all x5, blocking collectives, copies(): return lax.all_to_all(sent, axis, split_axis=0, concat_axis=0)  74.2 us
    all_to_all x1, waiting for transfers between devices, copies(): return lax.all_to_all(sent, axis, split_axis=0, concat_axis=0)  53.3 us
    all_gather x1, waiting for transfers between devices, body(): data_all = lax.all_gather(data, 'row', axis=0)  17.8 us
    all_to_all x1, waiting for transfers between devices, body(): plan = lax.all_to_all(plan, 'col', split_axis=0, concat_axis=0)  15.9 us
    all_to_all x1, blocking collectives, body(): pack = lax.all_to_all(pack, 'col', split_axis=0, concat_axis=0)  15.6 us
    all_to_all x1, starting transfers between devices, copies(): return lax.all_to_all(sent, axis, split_axis=0, concat_axis=0)  7.64 us
    pallas_call x1, Pallas kernels, body(): pl.pallas_call(functools.partial(cost_kernel, scale), out_shape=[jax.Shap...  5.9 us
  transfers between devices with their start and end apart: 4, of which 3 were waited for; matrix products, arithmetic and copies ran while one was open for 6% of the time, Pallas kernels for 0%

profile of v5, /device:TPU:1, one launch (start us, length us, event | category | flops | bytes accessed | tf_op | source)
XLA Modules:
  0.0 226.9 jit_solution(1905667997856325680)
XLA Ops:
  7.2 0.7 all-gather.5.cloned.1.call-update
  7.9 1.1 copy.17
  9.0 2.8 %broadcast_in_dim.14 = bf16[16,1024,128]{2,1,0:T(8,128)(2,1)} broadcast(bf16[1024,128]{1,0:T(8,128)(2,1)S(1)} %copy.17), dimensions={1,2} | broadcast | bytes 4456448 | tf_op jit(solution)/shard_map/broadcast_in_dim | solution.py:25
  11.8 7.6 %all-to-all-start = ((bf16[16,1024,128]{2,1,0:T(8,128)(2,1)}), bf16[16,1024,128]{2,1,0:T(8,128)(2,1)}, u32[]{:S(2)}, u32[]{:S(2)}) async-start(bf16[16,1024,128]{2,1,0:T(8,128)(2,1)} %broadcast_in_dim.14), calls=%async_computation | async-start | bytes 8388608 | tf_op jit(solution)/shard_map/all_to_all | solution.py:26
  19.6 53.3 %all-to-all-done.noise_hbm = bf16[16,1024,128]{2,1,0:T(8,128)(2,1)} async-done(((bf16[16,1024,128]{2,1,0:T(8,128)(2,1)}), bf16[16,1024,128]{2,1,0:T(8,128)(2,1)}, u32[]{:S(2)}, u32[]{:S(2)}) %all-to-all-start) | async-done | bytes 4194336 | tf_op jit(solution)/shard_map/all_to_all | solution.py:26
  72.9 4.4 %multiply_reduce_fusion = f32[128]{0:T(128)S(1)} fusion(bf16[16,1024,128]{2,1,0:T(8,128)(2,1)} %all-to-all-done.noise_hbm), kind=kLoop, calls=%fused_computation | loop fusion | flops 6291328 | bytes 4194816 | tf_op jit(solution)/shard_map/reduce_sum | solution.py:132
  77.3 17.8 %all-gather.5.cloned.1.call-done = bf16[8192,512]{1,0:T(8,128)(2,1)} async-done(((bf16[256,512]{1,0:T(8,128)(2,1)}), bf16[8192,512]{1,0:T(8,128)(2,1)}) %all-gather.5.cloned.1.call-update) | async-done | bytes 8388624 | tf_op jit(solution)/shard_map/all_gather | solution.py:130
  95.1 5.9 %cost.1 = (f32[128,256]{1,0:T(8,128)S(1)}, bf16[16,16,640]{2,1,0:T(8,128)(2,1)S(1)}) custom-call(s32[2]{0:T(128)S(1)} %pad_add_fusion.place_ref, bf16[16,1024,128]{2,1,0:T(8,128)(2,1)} %all-to-all-done.noise_hbm, bf16[32,256,512]{2,1,0:T(8,128)(2,1)} %bitcast.12, f32[1,128]{1,0:T(1,128)S(1)} %bitcast.10), custom_call_target="tpu_custom_call" | custom-call | flops 1073741824 | bytes 12582912 | tf_op jit(solution)/shard_map/cost/pallas_call | solution.py:135
  101.0 15.6 %all_to_all.40 = bf16[16,16,640]{2,1,0:T(8,128)(2,1)} all-to-all(bf16[16,16,640]{2,1,0:T(8,128)(2,1)S(1)} %get-tuple-element.13), channel_id=1, replica_groups=mesh['row'=32,'col'=16] {'col'}, dimensions={0} | all-to-all | bytes 655360 | tf_op jit(solution)/shard_map/all_to_all | solution.py:155
  116.6 0.8 convert_reduce_fusion
  117.4 0.1 add_reduce_fusion.3
  117.5 0.1 exponential_reduce_fusion.4
  117.7 21.0 %all_to_all.41 = f32[32,1,256]{2,1,0:T(1,128)S(1)} all-to-all(f32[32,1,256]{2,1,0:T(1,128)S(1)} %broadcast_in_dim.15), channel_id=1, replica_groups=mesh['row'=32,'col'=16] {'row'}, dimensions={0} | all-to-all | bytes 65536 | tf_op jit(solution)/shard_map/all_to_all | solution.py:26
  138.7 0.1 add_reduce_fusion.2
  138.9 0.2 exponential_reduce_fusion.3
  139.1 9.0 %all_to_all.42 = f32[16,1,128]{2,1,0:T(1,128)S(1)} all-to-all(f32[16,1,128]{2,1,0:T(1,128)S(1)} %broadcast_in_dim.16), channel_id=1, replica_groups=mesh['row'=32,'col'=16] {'col'}, dimensions={0} | all-to-all | bytes 16384 | tf_op jit(solution)/shard_map/all_to_all | solution.py:26
  148.2 0.1 add_reduce_fusion.1
  148.3 0.1 exponential_reduce_fusion.2
  148.5 18.2 %all_to_all.43 = f32[32,1,256]{2,1,0:T(1,128)S(1)} all-to-all(f32[32,1,256]{2,1,0:T(1,128)S(1)} %broadcast_in_dim.17), channel_id=1, replica_groups=mesh['row'=32,'col'=16] {'row'}, dimensions={0} | all-to-all | bytes 65536 | tf_op jit(solution)/shard_map/all_to_all | solution.py:26
  166.7 0.1 add_reduce_fusion
  166.8 0.2 exponential_reduce_fusion.1
  167.0 9.0 %all_to_all.44 = f32[16,1,128]{2,1,0:T(1,128)S(1)} all-to-all(f32[16,1,128]{2,1,0:T(1,128)S(1)} %broadcast_in_dim.18), channel_id=1, replica_groups=mesh['row'=32,'col'=16] {'col'}, dimensions={0} | all-to-all | bytes 16384 | tf_op jit(solution)/shard_map/all_to_all | solution.py:26
  176.1 0.5 broadcast_multiply_fusion.2
  176.6 0.1 add_reduce_fusion.4
  176.7 0.1 exponential_reduce_fusion
  176.9 17.1 %all_to_all.45 = f32[32,1,256]{2,1,0:T(1,128)S(1)} all-to-all(f32[32,1,256]{2,1,0:T(1,128)S(1)} %broadcast_in_dim.19), channel_id=1, replica_groups=mesh['row'=32,'col'=16] {'row'}, dimensions={0} | all-to-all | bytes 65536 | tf_op jit(solution)/shard_map/all_to_all | solution.py:26
  194.0 0.6 broadcast_multiply_fusion.1
  194.6 0.1 exponential_convert_fusion
  194.7 1.1 broadcast_in_dim.20
  195.8 3.9 %all-to-all-start.7 = ((bf16[16,128,256]{2,1,0:T(8,128)(2,1)}), bf16[16,128,256]{2,1,0:T(8,128)(2,1)S(1)}, u32[]{:S(2)}, u32[]{:S(2)}) async-start(bf16[16,128,256]{2,1,0:T(8,128)(2,1)} %broadcast_in_dim.20), calls=%async_computation.7 | async-start | bytes 2097152 | tf_op jit(solution)/shard_map/all_to_all | solution.py:171
  199.7 15.9 %all-to-all-done.7.plan_ref = bf16[16,128,256]{2,1,0:T(8,128)(2,1)S(1)} async-done(((bf16[16,128,256]{2,1,0:T(8,128)(2,1)}), bf16[16,128,256]{2,1,0:T(8,128)(2,1)S(1)}, u32[]{:S(2)}, u32[]{:S(2)}) %all-to-all-start.7) | async-done | bytes 1048608 | tf_op jit(solution)/shard_map/all_to_all | solution.py:171
  215.5 4.6 %plan.1 = bf16[128,1024]{1,0:T(8,128)(2,1)} custom-call(bf16[16,128,256]{2,1,0:T(8,128)(2,1)S(1)} %all-to-all-done.7.plan_ref, bf16[16,2,16,16,640]{4,3,2,1,0:T(8,128)(2,1)} %bitcast.11), custom_call_target="tpu_custom_call" | custom-call | tf_op jit(solution)/shard_map/plan/pallas_call | solution.py:172
  (31 shorter events, 0.7 us)
Async XLA Ops:
  7.2 87.9 %all-gather.5.cloned.1.call-start = ((), (), s32[]{:S(2)}) async-start(), calls=%async_computation.8 | async-start | bytes 8650752 | tf_op jit(solution)/shard_map/all_gather | solution.py:130
  11.8 61.1 %all-to-all-start = ((bf16[16,1024,128]{2,1,0:T(8,128)(2,1)}), bf16[16,1024,128]{2,1,0:T(8,128)(2,1)}, u32[]{:S(2)}, u32[]{:S(2)}) async-start(bf16[16,1024,128]{2,1,0:T(8,128)(2,1)} %broadcast_in_dim.14), calls=%async_computation | async-start | bytes 8388608 | tf_op jit(solution)/shard_map/all_to_all | solution.py:26
  19.4 180.2 %all-gather.7.cloned.1.call-start = ((), (), s32[]{:S(2)}) async-start(), calls=%async_computation.9 | async-start | bytes 10813440 | tf_op jit(solution)/shard_map/all_gather | solution.py:158
  195.8 19.7 %all-to-all-start.7 = ((bf16[16,128,256]{2,1,0:T(8,128)(2,1)}), bf16[16,128,256]{2,1,0:T(8,128)(2,1)S(1)}, u32[]{:S(2)}, u32[]{:S(2)}) async-start(bf16[16,128,256]{2,1,0:T(8,128)(2,1)} %broadcast_in_dim.20), calls=%async_computation.7 | async-start | bytes 2097152 | tf_op jit(solution)/shard_map/all_to_all | solution.py:171
Sparse Core Ops, SparseCore 0:
  10.1 84.9 all-gather.4
  116.7 78.5 all-gather.6

commit v6 on v5

--- a/solution.py
+++ b/solution.py
@@ -86,6 +86,15 @@
     tail = jnp.where(place == 0, head, jnp.where(place == 1, middle, rest)).astype(BF16)
     for c in range(blocks):
         pack_ref[c, :, depth:] = tail
+
+
+def spread_kernel(scale, shift, cost_ref, u_ref, v_ref, out_ref):
+    rows, cols = cost_ref.shape
+    u = jnp.broadcast_to(u_ref[...], (rows, rows)).T
+    u = jnp.concatenate([u] * (cols // rows), axis=1)
+    plan = jnp.exp(cost_ref[...] * scale + u + v_ref[...] + shift).astype(BF16)
+    for c in range(out_ref.shape[0]):
+        out_ref[c] = plan
 
 
 def plan_kernel(plan_ref, data_hbm, out_ref, data_ref, acc_ref, sems):
@@ -165,8 +174,14 @@
         parts = copies(local.reshape(1, cols), "row", ROWS)
         v = -log_cols - log_sum_exp(parts, 0).reshape(cols)
 
-    plan = jnp.exp(scores + u[:, None] + v[None, :] + log_rows).astype(BF16)
-    plan = jnp.broadcast_to(plan[None], (COLS, rows, cols))
+    plan = pl.pallas_call(
+        functools.partial(spread_kernel, scale, log_rows),
+        out_shape=jax.ShapeDtypeStruct((COLS, rows, cols), BF16),
+        in_specs=[VM] * 3,
+        out_specs=VM,
+        compiler_params=pltpu.CompilerParams(vmem_limit_bytes=16 * MIB),
+        name="spread",
+    )(cost, u.reshape(1, rows), v.reshape(1, cols))
     values, _ = lax.optimization_barrier((values, plan))
     plan = lax.all_to_all(plan, "col", split_axis=0, concat_axis=0)
     targets = pl.pallas_call(

time: 228 us -> 228 us (level)
  transfers between devices with their start and end apart: 4 -> 4, of which waited for: 3 -> 3; matrix products, arithmetic and copies ran while one was open for 6% -> 5% of each run, Pallas kernels for 0% -> 1%
where the time goes in v6:
time: 228 us; the launch traced here: 227 us
  blocking collectives  89.8 us (39%)
  waiting for transfers between devices  87.6 us (38%)
  between operations  14.2 us (6%)
  starting transfers between devices  11.6 us (5%)
  Pallas kernels  11.6 us (5%)
  other arithmetic  8.11 us (4%)
  local copies, waits for them, and re-layouts  3.97 us (2%)
    all_to_all x5, blocking collectives, copies(): return lax.all_to_all(sent, axis, split_axis=0, concat_axis=0)  74.2 us
    all_to_all x1, waiting for transfers between devices, copies(): return lax.all_to_all(sent, axis, split_axis=0, concat_axis=0)  53.3 us
    all_gather x1, waiting for transfers between devices, body(): data_all = lax.all_gather(data, 'row', axis=0)  17.8 us
    all_to_all x1, waiting for transfers between devices, body(): plan = lax.all_to_all(plan, 'col', split_axis=0, concat_axis=0)  15.9 us
    all_to_all x1, blocking collectives, body(): pack = lax.all_to_all(pack, 'col', split_axis=0, concat_axis=0)  15.6 us
    all_to_all x1, starting transfers between devices, copies(): return lax.all_to_all(sent, axis, split_axis=0, concat_axis=0)  7.64 us
    pallas_call x1, Pallas kernels, body(): pl.pallas_call(functools.partial(cost_kernel, scale), out_shape=[jax.Shap...  5.9 us
  transfers between devices with their start and end apart: 4, of which 3 were waited for; matrix products, arithmetic and copies ran while one was open for 5% of the time, Pallas kernels for 1%

profile of v6, /device:TPU:1, one launch (start us, length us, event | category | flops | bytes accessed | tf_op | source)
XLA Modules:
  0.0 226.9 jit_solution(10817647134028653759)
XLA Ops:
  7.2 0.7 all-gather.5.cloned.1.call-update
  7.9 1.1 copy.17
  9.0 2.8 %broadcast_in_dim.12 = bf16[16,1024,128]{2,1,0:T(8,128)(2,1)} broadcast(bf16[1024,128]{1,0:T(8,128)(2,1)S(1)} %copy.17), dimensions={1,2} | broadcast | bytes 4456448 | tf_op jit(solution)/shard_map/broadcast_in_dim | solution.py:25
  11.8 7.6 %all-to-all-start = ((bf16[16,1024,128]{2,1,0:T(8,128)(2,1)}), bf16[16,1024,128]{2,1,0:T(8,128)(2,1)}, u32[]{:S(2)}, u32[]{:S(2)}) async-start(bf16[16,1024,128]{2,1,0:T(8,128)(2,1)} %broadcast_in_dim.12), calls=%async_computation | async-start | bytes 8388608 | tf_op jit(solution)/shard_map/all_to_all | solution.py:26
  19.5 0.1 pad_add_fusion.place_ref
  19.6 53.3 %all-to-all-done.noise_hbm = bf16[16,1024,128]{2,1,0:T(8,128)(2,1)} async-done(((bf16[16,1024,128]{2,1,0:T(8,128)(2,1)}), bf16[16,1024,128]{2,1,0:T(8,128)(2,1)}, u32[]{:S(2)}, u32[]{:S(2)}) %all-to-all-start) | async-done | bytes 4194336 | tf_op jit(solution)/shard_map/all_to_all | solution.py:26
  72.9 4.4 %multiply_reduce_fusion = f32[128]{0:T(128)S(1)} fusion(bf16[16,1024,128]{2,1,0:T(8,128)(2,1)} %all-to-all-done.noise_hbm), kind=kLoop, calls=%fused_computation | loop fusion | flops 6291328 | bytes 4194816 | tf_op jit(solution)/shard_map/reduce_sum | solution.py:141
  77.3 17.8 %all-gather.5.cloned.1.call-done = bf16[8192,512]{1,0:T(8,128)(2,1)} async-done(((bf16[256,512]{1,0:T(8,128)(2,1)}), bf16[8192,512]{1,0:T(8,128)(2,1)}) %all-gather.5.cloned.1.call-update) | async-done | bytes 8388624 | tf_op jit(solution)/shard_map/all_gather | solution.py:139
  95.1 5.9 %cost.1 = (f32[128,256]{1,0:T(8,128)S(1)}, bf16[16,16,640]{2,1,0:T(8,128)(2,1)S(1)}) custom-call(s32[2]{0:T(128)S(1)} %pad_add_fusion.place_ref, bf16[16,1024,128]{2,1,0:T(8,128)(2,1)} %all-to-all-done.noise_hbm, bf16[32,256,512]{2,1,0:T(8,128)(2,1)} %bitcast.16, f32[1,128]{1,0:T(1,128)S(1)} %bitcast.14), custom_call_target="tpu_custom_call" | custom-call | flops 1073741824 | bytes 12582912 | tf_op jit(solution)/shard_map/cost/pallas_call | solution.py:144
  101.0 15.6 %all_to_all.40 = bf16[16,16,640]{2,1,0:T(8,128)(2,1)} all-to-all(bf16[16,16,640]{2,1,0:T(8,128)(2,1)S(1)} %get-tuple-element.13), channel_id=1, replica_groups=mesh['row'=32,'col'=16] {'col'}, dimensions={0} | all-to-all | bytes 655360 | tf_op jit(solution)/shard_map/all_to_all | solution.py:164
  116.6 0.8 convert_reduce_fusion
  117.4 0.1 add_reduce_fusion.4
  117.5 0.1 exponential_reduce_fusion.4
  117.7 21.0 %all_to_all.41 = f32[32,1,256]{2,1,0:T(1,128)S(1)} all-to-all(f32[32,1,256]{2,1,0:T(1,128)S(1)} %broadcast_in_dim.13), channel_id=1, replica_groups=mesh['row'=32,'col'=16] {'row'}, dimensions={0} | all-to-all | bytes 65536 | tf_op jit(solution)/shard_map/all_to_all | solution.py:26
  138.7 0.1 add_reduce_fusion.3
  138.9 0.2 exponential_reduce_fusion.3
  139.1 9.0 %all_to_all.42 = f32[16,1,128]{2,1,0:T(1,128)S(1)} all-to-all(f32[16,1,128]{2,1,0:T(1,128)S(1)} %broadcast_in_dim.14), channel_id=1, replica_groups=mesh['row'=32,'col'=16] {'col'}, dimensions={0} | all-to-all | bytes 16384 | tf_op jit(solution)/shard_map/all_to_all | solution.py:26
  148.2 0.1 add_reduce_fusion.2
  148.3 0.1 exponential_reduce_fusion.2
  148.5 18.2 %all_to_all.43 = f32[32,1,256]{2,1,0:T(1,128)S(1)} all-to-all(f32[32,1,256]{2,1,0:T(1,128)S(1)} %broadcast_in_dim.15), channel_id=1, replica_groups=mesh['row'=32,'col'=16] {'row'}, dimensions={0} | all-to-all | bytes 65536 | tf_op jit(solution)/shard_map/all_to_all | solution.py:26
  166.7 0.1 add_reduce_fusion.1
  166.8 0.2 exponential_reduce_fusion.1
  167.0 9.0 %all_to_all.44 = f32[16,1,128]{2,1,0:T(1,128)S(1)} all-to-all(f32[16,1,128]{2,1,0:T(1,128)S(1)} %broadcast_in_dim.16), channel_id=1, replica_groups=mesh['row'=32,'col'=16] {'col'}, dimensions={0} | all-to-all | bytes 16384 | tf_op jit(solution)/shard_map/all_to_all | solution.py:26
  176.1 0.5 broadcast_multiply_fusion.2
  176.6 0.1 add_reduce_fusion
  176.7 0.1 exponential_reduce_fusion
  176.9 17.1 %all_to_all.45 = f32[32,1,256]{2,1,0:T(1,128)S(1)} all-to-all(f32[32,1,256]{2,1,0:T(1,128)S(1)} %broadcast_in_dim.17), channel_id=1, replica_groups=mesh['row'=32,'col'=16] {'row'}, dimensions={0} | all-to-all | bytes 65536 | tf_op jit(solution)/shard_map/all_to_all | solution.py:26
  194.0 0.6 broadcast_multiply_fusion.1
  194.6 1.2 spread.1
  195.8 3.8 %all-to-all-start.7 = ((bf16[16,128,256]{2,1,0:T(8,128)(2,1)}), bf16[16,128,256]{2,1,0:T(8,128)(2,1)S(1)}, u32[]{:S(2)}, u32[]{:S(2)}) async-start(bf16[16,128,256]{2,1,0:T(8,128)(2,1)} %spread.1), calls=%async_computation.7 | async-start | bytes 2097152 | tf_op jit(solution)/shard_map/all_to_all | solution.py:186
  199.6 15.9 %all-to-all-done.7.plan_ref = bf16[16,128,256]{2,1,0:T(8,128)(2,1)S(1)} async-done(((bf16[16,128,256]{2,1,0:T(8,128)(2,1)}), bf16[16,128,256]{2,1,0:T(8,128)(2,1)S(1)}, u32[]{:S(2)}, u32[]{:S(2)}) %all-to-all-start.7) | async-done | bytes 1048608 | tf_op jit(solution)/shard_map/all_to_all | solution.py:186
  215.5 4.6 %plan.1 = bf16[128,1024]{1,0:T(8,128)(2,1)} custom-call(bf16[16,128,256]{2,1,0:T(8,128)(2,1)S(1)} %all-to-all-done.7.plan_ref, bf16[16,2,16,16,640]{4,3,2,1,0:T(8,128)(2,1)} %bitcast.15), custom_call_target="tpu_custom_call" | custom-call | tf_op jit(solution)/shard_map/plan/pallas_call | solution.py:187
  (30 shorter events, 0.7 us)
Async XLA Ops:
  7.2 87.9 %all-gather.5.cloned.1.call-start = ((), (), s32[]{:S(2)}) async-start(), calls=%async_computation.8 | async-start | bytes 8650752 | tf_op jit(solution)/shard_map/all_gather | solution.py:139
  11.8 61.1 %all-to-all-start = ((bf16[16,1024,128]{2,1,0:T(8,128)(2,1)}), bf16[16,1024,128]{2,1,0:T(8,128)(2,1)}, u32[]{:S(2)}, u32[]{:S(2)}) async-start(bf16[16,1024,128]{2,1,0:T(8,128)(2,1)} %broadcast_in_dim.12), calls=%async_computation | async-start | bytes 8388608 | tf_op jit(solution)/shard_map/all_to_all | solution.py:26
  19.4 180.2 %all-gather.7.cloned.1.call-start = ((), (), s32[]{:S(2)}) async-start(), calls=%async_computation.9 | async-start | bytes 10813440 | tf_op jit(solution)/shard_map/all_gather | solution.py:167
  195.8 19.7 %all-to-all-start.7 = ((bf16[16,128,256]{2,1,0:T(8,128)(2,1)}), bf16[16,128,256]{2,1,0:T(8,128)(2,1)S(1)}, u32[]{:S(2)}, u32[]{:S(2)}) async-start(bf16[16,128,256]{2,1,0:T(8,128)(2,1)} %spread.1), calls=%async_computation.7 | async-start | bytes 2097152 | tf_op jit(solution)/shard_map/all_to_all | solution.py:186
Sparse Core Ops, SparseCore 0:
  10.1 84.9 all-gather.4
  116.7 78.5 all-gather.6

commit v7 on v6

--- a/solution.py
+++ b/solution.py
@@ -88,7 +88,9 @@
         pack_ref[c, :, depth:] = tail
 
 
-def spread_kernel(scale, shift, cost_ref, u_ref, v_ref, out_ref):
+def spread_kernel(scale, shift, cost_ref, u_ref, v_ref, out_ref, row_ref, col_ref):
+    row_ref[...] = EPS * u_ref[...]
+    col_ref[...] = EPS * v_ref[...]
     rows, cols = cost_ref.shape
     u = jnp.broadcast_to(u_ref[...], (rows, rows)).T
     u = jnp.concatenate([u] * (cols // rows), axis=1)
@@ -174,11 +176,15 @@
         parts = copies(local.reshape(1, cols), "row", ROWS)
         v = -log_cols - log_sum_exp(parts, 0).reshape(cols)
 
-    plan = pl.pallas_call(
+    plan, row_potential, col_potential = pl.pallas_call(
         functools.partial(spread_kernel, scale, log_rows),
-        out_shape=jax.ShapeDtypeStruct((COLS, rows, cols), BF16),
+        out_shape=[
+            jax.ShapeDtypeStruct((COLS, rows, cols), BF16),
+            jax.ShapeDtypeStruct((1, rows), F32),
+            jax.ShapeDtypeStruct((1, cols), F32),
+        ],
         in_specs=[VM] * 3,
-        out_specs=VM,
+        out_specs=[VM] * 3,
         compiler_params=pltpu.CompilerParams(vmem_limit_bytes=16 * MIB),
         name="spread",
     )(cost, u.reshape(1, rows), v.reshape(1, cols))
@@ -197,7 +203,7 @@
         compiler_params=pltpu.CompilerParams(vmem_limit_bytes=50 * MIB),
         name="plan",
     )(plan, values)
-    return (targets, EPS * u, EPS * v)
+    return (targets, row_potential.reshape(rows), col_potential.reshape(cols))
 
 
 def solution(mesh):

time: 228 us -> 226 us (level)
  no operation moved by 1% of the time
where the time goes in v7:
time: 226 us
  blocking collectives  89.7 us (40%)
  waiting for transfers between devices  87.7 us (39%)
  between operations  14.2 us (6%)
  Pallas kernels  11.6 us (5%)
  starting transfers between devices  11.5 us (5%)
  other arithmetic  7.04 us (3%)
  local copies, waits for them, and re-layouts  3.97 us (2%)
    all_to_all x5, blocking collectives, copies(): return lax.all_to_all(sent, axis, split_axis=0, concat_axis=0)  74.2 us
    all_to_all x1, waiting for transfers between devices, copies(): return lax.all_to_all(sent, axis, split_axis=0, concat_axis=0)  53.3 us
    all_gather x1, waiting for transfers between devices, body(): data_all = lax.all_gather(data, 'row', axis=0)  17.8 us
    all_to_all x1, waiting for transfers between devices, body(): plan = lax.all_to_all(plan, 'col', split_axis=0, concat_axis=0)  15.9 us
    all_to_all x1, blocking collectives, body(): pack = lax.all_to_all(pack, 'col', split_axis=0, concat_axis=0)  15.6 us
    all_to_all x1, starting transfers between devices, copies(): return lax.all_to_all(sent, axis, split_axis=0, concat_axis=0)  7.64 us
    pallas_call x1, Pallas kernels, body(): pl.pallas_call(functools.partial(cost_kernel, scale), out_shape=[jax.Shap...  5.9 us
    pallas_call x1, Pallas kernels, body(): pl.pallas_call(plan_kernel, out_shape=jax.ShapeDtypeStruct((rows, width),...  4.56 us
  transfers between devices with their start and end apart: 4, of which 3 were waited for; matrix products, arithmetic and copies ran while one was open for 5% of the time, Pallas kernels for 1%

profile of v7, /device:TPU:1, one launch (start us, length us, event | category | flops | bytes accessed | tf_op | source)
XLA Modules:
  0.0 225.8 jit_solution(9073107858904814054)
XLA Ops:
  7.2 0.7 all-gather.5.cloned.1.call-update
  7.9 1.1 copy.17
  9.0 2.8 %broadcast_in_dim.12 = bf16[16,1024,128]{2,1,0:T(8,128)(2,1)} broadcast(bf16[1024,128]{1,0:T(8,128)(2,1)S(1)} %copy.17), dimensions={1,2} | broadcast | bytes 4456448 | tf_op jit(solution)/shard_map/broadcast_in_dim | solution.py:25
  11.8 7.6 %all-to-all-start = ((bf16[16,1024,128]{2,1,0:T(8,128)(2,1)}), bf16[16,1024,128]{2,1,0:T(8,128)(2,1)}, u32[]{:S(2)}, u32[]{:S(2)}) async-start(bf16[16,1024,128]{2,1,0:T(8,128)(2,1)} %broadcast_in_dim.12), calls=%async_computation | async-start | bytes 8388608 | tf_op jit(solution)/shard_map/all_to_all | solution.py:26
  19.5 0.1 pad_add_fusion.place_ref
  19.6 53.3 %all-to-all-done.noise_hbm = bf16[16,1024,128]{2,1,0:T(8,128)(2,1)} async-done(((bf16[16,1024,128]{2,1,0:T(8,128)(2,1)}), bf16[16,1024,128]{2,1,0:T(8,128)(2,1)}, u32[]{:S(2)}, u32[]{:S(2)}) %all-to-all-start) | async-done | bytes 4194336 | tf_op jit(solution)/shard_map/all_to_all | solution.py:26
  72.9 4.4 %multiply_reduce_fusion = f32[128]{0:T(128)S(1)} fusion(bf16[16,1024,128]{2,1,0:T(8,128)(2,1)} %all-to-all-done.noise_hbm), kind=kLoop, calls=%fused_computation | loop fusion | flops 6291328 | bytes 4194816 | tf_op jit(solution)/shard_map/reduce_sum | solution.py:143
  77.3 17.8 %all-gather.5.cloned.1.call-done = bf16[8192,512]{1,0:T(8,128)(2,1)} async-done(((bf16[256,512]{1,0:T(8,128)(2,1)}), bf16[8192,512]{1,0:T(8,128)(2,1)}) %all-gather.5.cloned.1.call-update) | async-done | bytes 8388624 | tf_op jit(solution)/shard_map/all_gather | solution.py:141
  95.1 5.9 %cost.1 = (f32[128,256]{1,0:T(8,128)S(1)}, bf16[16,16,640]{2,1,0:T(8,128)(2,1)S(1)}) custom-call(s32[2]{0:T(128)S(1)} %pad_add_fusion.place_ref, bf16[16,1024,128]{2,1,0:T(8,128)(2,1)} %all-to-all-done.noise_hbm, bf16[32,256,512]{2,1,0:T(8,128)(2,1)} %bitcast.18, f32[1,128]{1,0:T(1,128)S(1)} %bitcast.16), custom_call_target="tpu_custom_call" | custom-call | flops 1073741824 | bytes 12582912 | tf_op jit(solution)/shard_map/cost/pallas_call | solution.py:146
  101.0 15.6 %all_to_all.40 = bf16[16,16,640]{2,1,0:T(8,128)(2,1)} all-to-all(bf16[16,16,640]{2,1,0:T(8,128)(2,1)S(1)} %get-tuple-element.16), channel_id=1, replica_groups=mesh['row'=32,'col'=16] {'col'}, dimensions={0} | all-to-all | bytes 655360 | tf_op jit(solution)/shard_map/all_to_all | solution.py:166
  116.6 0.8 convert_reduce_fusion
  117.4 0.1 add_reduce_fusion.4
  117.5 0.1 exponential_reduce_fusion.4
  117.7 21.0 %all_to_all.41 = f32[32,1,256]{2,1,0:T(1,128)S(1)} all-to-all(f32[32,1,256]{2,1,0:T(1,128)S(1)} %broadcast_in_dim.13), channel_id=1, replica_groups=mesh['row'=32,'col'=16] {'row'}, dimensions={0} | all-to-all | bytes 65536 | tf_op jit(solution)/shard_map/all_to_all | solution.py:26
  138.7 0.1 reduce_max.101
  138.7 0.1 add_reduce_fusion.3
  138.9 0.2 exponential_reduce_fusion.3
  139.1 9.0 %all_to_all.42 = f32[16,1,128]{2,1,0:T(1,128)S(1)} all-to-all(f32[16,1,128]{2,1,0:T(1,128)S(1)} %broadcast_in_dim.14), channel_id=1, replica_groups=mesh['row'=32,'col'=16] {'col'}, dimensions={0} | all-to-all | bytes 16384 | tf_op jit(solution)/shard_map/all_to_all | solution.py:26
  148.2 0.1 add_reduce_fusion.2
  148.3 0.1 exponential_reduce_fusion.2
  148.5 18.2 %all_to_all.43 = f32[32,1,256]{2,1,0:T(1,128)S(1)} all-to-all(f32[32,1,256]{2,1,0:T(1,128)S(1)} %broadcast_in_dim.15), channel_id=1, replica_groups=mesh['row'=32,'col'=16] {'row'}, dimensions={0} | all-to-all | bytes 65536 | tf_op jit(solution)/shard_map/all_to_all | solution.py:26
  166.6 0.1 reduce_max.105
  166.7 0.1 add_reduce_fusion.1
  166.8 0.2 exponential_reduce_fusion.1
  167.0 9.0 %all_to_all.44 = f32[16,1,128]{2,1,0:T(1,128)S(1)} all-to-all(f32[16,1,128]{2,1,0:T(1,128)S(1)} %broadcast_in_dim.16), channel_id=1, replica_groups=mesh['row'=32,'col'=16] {'col'}, dimensions={0} | all-to-all | bytes 16384 | tf_op jit(solution)/shard_map/all_to_all | solution.py:26
  176.1 0.1 add_reduce_fusion
  176.2 0.1 exponential_reduce_fusion
  176.4 17.0 %all_to_all.45 = f32[32,1,256]{2,1,0:T(1,128)S(1)} all-to-all(f32[32,1,256]{2,1,0:T(1,128)S(1)} %broadcast_in_dim.17), channel_id=1, replica_groups=mesh['row'=32,'col'=16] {'row'}, dimensions={0} | all-to-all | bytes 65536 | tf_op jit(solution)/shard_map/all_to_all | solution.py:26
  193.5 1.2 spread.1
  194.7 3.7 %all-to-all-start.7 = ((bf16[16,128,256]{2,1,0:T(8,128)(2,1)}), bf16[16,128,256]{2,1,0:T(8,128)(2,1)S(1)}, u32[]{:S(2)}, u32[]{:S(2)}) async-start(bf16[16,128,256]{2,1,0:T(8,128)(2,1)} %get-tuple-element.17), calls=%async_computation.7 | async-start | bytes 2097152 | tf_op jit(solution)/shard_map/all_to_all | solution.py:192
  198.4 15.9 %all-to-all-done.7.plan_ref = bf16[16,128,256]{2,1,0:T(8,128)(2,1)S(1)} async-done(((bf16[16,128,256]{2,1,0:T(8,128)(2,1)}), bf16[16,128,256]{2,1,0:T(8,128)(2,1)S(1)}, u32[]{:S(2)}, u32[]{:S(2)}) %all-to-all-start.7) | async-done | bytes 1048608 | tf_op jit(solution)/shard_map/all_to_all | solution.py:192
  214.4 4.6 %plan.1 = bf16[128,1024]{1,0:T(8,128)(2,1)} custom-call(bf16[16,128,256]{2,1,0:T(8,128)(2,1)S(1)} %all-to-all-done.7.plan_ref, bf16[16,2,16,16,640]{4,3,2,1,0:T(8,128)(2,1)} %bitcast.17), custom_call_target="tpu_custom_call" | custom-call | tf_op jit(solution)/shard_map/plan/pallas_call | solution.py:193
  (30 shorter events, 0.6 us)
Async XLA Ops:
  7.2 87.9 %all-gather.5.cloned.1.call-start = ((), (), s32[]{:S(2)}) async-start(), calls=%async_computation.8 | async-start | bytes 8650752 | tf_op jit(solution)/shard_map/all_gather | solution.py:141
  11.8 61.1 %all-to-all-start = ((bf16[16,1024,128]{2,1,0:T(8,128)(2,1)}), bf16[16,1024,128]{2,1,0:T(8,128)(2,1)}, u32[]{:S(2)}, u32[]{:S(2)}) async-start(bf16[16,1024,128]{2,1,0:T(8,128)(2,1)} %broadcast_in_dim.12), calls=%async_computation | async-start | bytes 8388608 | tf_op jit(solution)/shard_map/all_to_all | solution.py:26
  19.4 179.0 %all-gather.7.cloned.1.call-start = ((), (), s32[]{:S(2)}) async-start(), calls=%async_computation.9 | async-start | bytes 10813440 | tf_op jit(solution)/shard_map/all_gather | solution.py:169
  194.7 19.7 %all-to-all-start.7 = ((bf16[16,128,256]{2,1,0:T(8,128)(2,1)}), bf16[16,128,256]{2,1,0:T(8,128)(2,1)S(1)}, u32[]{:S(2)}, u32[]{:S(2)}) async-start(bf16[16,128,256]{2,1,0:T(8,128)(2,1)} %get-tuple-element.17), calls=%async_computation.7 | async-start | bytes 2097152 | tf_op jit(solution)/shard_map/all_to_all | solution.py:192
Sparse Core Ops, SparseCore 0:
  10.1 84.9 all-gather.4
  116.7 78.5 all-gather.6
